TPU v7x, 256 devices: a whole 4x4x8 slice. The times are simulated.
256 devices in a mesh: row: 8 (over x, core), col: 32 (over y, z).
Axes of the slice: x: 4, y: 4, z: 8, core: 2. Of those that a mesh axis runs over, the one named last changes fastest.
Arguments:
- normal: float32 [16384, 16384], P('row', 'col'), may hold values from -0.25 to 7.25, as said below
- jacobian: bfloat16 [512, 16384], P(None, ('row', 'col')), may hold values from -1 to 1
Outputs:
- updated: float32 [16384, 16384], P('row', 'col')
- panel: float32 [16384, 512], P('row', 'col')
Inputs may be any that keep to these rules, and one draw needn't show every extreme that they name: `normal`: in logical order of rows and columns the matrix is symmetric and positive definite.
All inputs are finite; a program needn't handle non-finite values.
Results may differ from a plain program's by a relative error of at most 0.00035.
Values may be sent and summed in bfloat16 or wider, within the bound.
No kernel may reach another device: no remote copies, remote signals or barrier semaphores. Data moves between devices by JAX's collectives and lax.ppermute only.
A program may use at most 128 MiB of HBM per device.

v0:
```python
import jax
import jax.numpy as jnp
from jax import lax
from jax.sharding import PartitionSpec as P

PW = 512
NB = 16


def from_root(value, axis, root):
    mine = lax.axis_index(axis) == root
    return lax.psum(jnp.where(mine, value, jnp.zeros_like(value)), axis)


def per_device(normal, jacobian):
    rows_loc, cols_loc = normal.shape
    row_count = lax.axis_size("row")
    col_count = lax.axis_size("col")
    col_pos = lax.axis_index("col")
    col_ratio = col_count // row_count
    per_row = PW // row_count
    per_col = PW // col_count
    batch = jacobian.shape[0]
    jac_rows = lax.all_gather(jacobian, "col", axis=1, tiled=True)
    shaped = jac_rows.reshape(batch, rows_loc // (col_ratio * NB), col_ratio, NB)
    my_cols = lax.dynamic_index_in_dim(shaped, col_pos // row_count, 2, keepdims=False).reshape(
        batch, cols_loc
    )
    jac_cols = from_root(my_cols, "row", col_pos % row_count)
    gram = normal + lax.dot_general(
        jac_rows, jac_cols, (((0,), (0,)), ((), ())), preferred_element_type=jnp.float32
    )
    corner = gram[:per_row, :per_col][None]
    diag_tiles = lax.all_gather(corner, ("row", "col"), axis=0, tiled=True)
    diag_tiles = diag_tiles.reshape(row_count, col_count, per_row // NB, NB, per_col // NB, NB)
    block = jnp.transpose(diag_tiles, (2, 0, 3, 4, 1, 5)).reshape(PW, PW)
    factor = jnp.linalg.cholesky(block)
    inverse = jax.scipy.linalg.solve_triangular(factor, jnp.eye(PW, dtype=jnp.float32), lower=True)
    inv_trans = inverse.T
    local_panel = gram[:, :per_col]
    piece_cols = lax.all_gather(local_panel, "col", axis=1, tiled=True)
    gathered_idx = jnp.arange(piece_cols.shape[1], dtype=jnp.int32)
    owner = gathered_idx // per_col
    within = gathered_idx % per_col
    rows_sel = jnp.take(inv_trans, (within // NB * col_count + owner) * NB + within % NB, axis=0)
    panel = jnp.dot(
        piece_cols, rows_sel, precision=lax.Precision.HIGHEST, preferred_element_type=jnp.float32
    )
    own_panel = lax.dynamic_slice_in_dim(panel, col_pos * per_col, per_col, 1)
    shaped_panel = panel.reshape(rows_loc // (col_ratio * NB), col_ratio, NB, PW)
    chosen = lax.dynamic_index_in_dim(
        shaped_panel, col_pos // row_count, 1, keepdims=False
    ).reshape(cols_loc, PW)
    far_rows = from_root(chosen, "row", col_pos % row_count)
    updated = gram - lax.dot_general(
        panel,
        far_rows,
        (((1,), (1,)), ((), ())),
        precision=lax.Precision.HIGHEST,
        preferred_element_type=jnp.float32,
    )
    return (updated, own_panel)


def solution(mesh):
    placed = (P("row", "col"), P(None, ("row", "col")))
    return jax.shard_map(
        per_device,
        mesh=mesh,
        in_specs=placed,
        out_specs=(P("row", "col"), P("row", "col")),
        check_vma=False,
    )
```

profile of v0, /device:TPU:1, one launch (start us, length us, event | category | flops | bytes accessed | tf_op | source)
XLA Modules:
  0.0 532.1 jit_solution(12143171105025864011)
XLA Ops:
  7.2 0.7 all-gather.6.cloned.1.call-update
  8.0 80.5 %all-gather.6.cloned.1.call-done = bf16[512,2048]{0,1:T(8,128)(2,1)} async-done(((bf16[512,64]{0,1:T(8,128)(2,1)}), bf16[512,2048]{0,1:T(8,128)(2,1)}) %all-gather.6.cloned.1.call-update) | async-done | bytes 2097168 | tf_op jit(solution)/shard_map/all_gather | solution.py:24
  88.5 1.9 dynamic-slice_select_fusion.1
  90.5 5.5 %copy.19 = f32[2048,512]{0,1:T(8,128)} copy(f32[2048,512]{1,0:T(8,128)} %param.2) | data formatting | bytes 8388608 | tf_op args[0]
  96.0 59.7 %all-reduce.4.cloned.1.call-done = bf16[512,512]{0,1:T(8,128)(2,1)} async-done(((bf16[512,512]{0,1:T(8,128)(2,1)}), bf16[512,512]{0,1:T(8,128)(2,1)}) %all-reduce.4.cloned.1.call-update) | async-done | bytes 524304 | tf_op jit(solution)/shard_map/psum | solution.py:12
  155.6 3.6 bitcast_add_fusion
  159.3 2.0 copy-done.1
  161.3 0.6 slice_bitcast_fusion.8
  161.9 1.6 slice.135
  163.7 0.1 iota_compare_fusion
  163.8 0.1 fusion.13
  163.9 103.9 %all-gather.10.cloned.1.call-done = f32[256,64,16]{1,2,0:T(8,128)} async-done(((f32[1,64,16]{1,2,0:T(8,128)}), f32[256,64,16]{1,2,0:T(8,128)}) %all-gather.10.cloned.1.call-update) | async-done | bytes 1048592 | tf_op jit(solution)/shard_map/all_gather | solution.py:34
  267.7 2.9 copy.20
  270.6 2.5 reshape.205
  273.1 7.0 %copy.21 = f32[4,8,16,1,32,16]{5,4,2,1,0,3:T(8,128)} copy(f32[4,8,16,1,32,16]{4,1,5,2,0,3:T(8,128)} %bitcast.72) | data formatting | bytes 2097152 | tf_op jit(solution)/shard_map/transpose | solution.py:36
  280.1 7.8 %reshape.206 = f32[512,512]{1,0:T(8,128)S(1)} reshape(f32[4,8,16,1,32,16]{5,4,2,1,0,3:T(8,128)} %copy.21) | data formatting | bytes 2097152 | tf_op jit(solution)/shard_map/reshape | solution.py:36
  287.8 0.3 copy.22
  288.2 0.2 fusion
  288.4 1.0 copy-done.3
  289.4 11.7 %cholesky.105 = f32[128,128]{1,0:T(8,128)S(1)} custom-call(f32[128,128]{1,0:T(8,128)S(1)} %cholesky.269), custom_call_target="Cholesky" | custom-call | tf_op jit(solution)/shard_map/jit(cholesky)/cholesky | solution.py:37
  301.1 0.1 cholesky.226
  301.3 9.8 %custom-call.31 = f32[1,128,128]{1,2,0:T(8,128)S(1)} custom-call(f32[1,128,128]{2,1,0:T(8,128)S(1)} %get-tuple-element.35), custom_call_target="InvertDiagBlocksLowerTriangular" | custom-call | tf_op jit(solution)/shard_map/jit(cholesky)/cholesky | solution.py:37
  311.1 1.2 constant_dynamic-update-slice_fusion.1
  312.3 1.3 convolution_subtract_fusion.4
  313.6 11.7 %cholesky.219 = f32[128,128]{1,0:T(8,128)S(1)} custom-call(f32[128,128]{1,0:T(8,128)S(1)} %cholesky.273), custom_call_target="Cholesky" | custom-call | tf_op jit(solution)/shard_map/jit(cholesky)/cholesky | solution.py:37
  325.4 10.0 %custom-call.32 = f32[1,128,128]{1,2,0:T(8,128)S(1)} custom-call(f32[1,128,128]{2,1,0:T(8,128)S(1)} %get-tuple-element.32), custom_call_target="InvertDiagBlocksLowerTriangular" | custom-call | tf_op jit(solution)/shard_map/jit(cholesky)/cholesky | solution.py:37
  335.4 0.3 convolution_dynamic-update-slice_fusion
  335.6 1.3 convolution_subtract_fusion.5
  336.9 11.7 %cholesky.240 = f32[128,128]{1,0:T(8,128)S(1)} custom-call(f32[128,128]{1,0:T(8,128)S(1)} %cholesky.278), custom_call_target="Cholesky" | custom-call | tf_op jit(solution)/shard_map/jit(cholesky)/cholesky | solution.py:37
  348.7 9.8 %custom-call.33 = f32[1,128,128]{1,2,0:T(8,128)S(1)} custom-call(f32[1,128,128]{2,1,0:T(8,128)S(1)} %get-tuple-element.29), custom_call_target="InvertDiagBlocksLowerTriangular" | custom-call | tf_op jit(solution)/shard_map/jit(cholesky)/cholesky | solution.py:37
  358.5 0.2 convolution_dynamic-update-slice_fusion.1
  358.7 1.2 convolution_subtract_fusion.6
  360.0 11.7 %cholesky.257 = f32[128,128]{1,0:T(8,128)S(1)} custom-call(f32[128,128]{1,0:T(8,128)S(1)} %convolution_subtract_fusion.6), custom_call_target="Cholesky" | custom-call | tf_op jit(solution)/shard_map/jit(cholesky)/cholesky | solution.py:37
  371.7 0.7 compare_reduce_fusion.2
  373.7 0.7 compare_reduce_fusion.1
  375.0 0.7 compare_reduce_fusion
  376.2 0.1 select_select_fusion
  376.4 11.0 %while.1 = (s32[]{:T(128)}, f32[512,512]{1,0:T(8,128)S(1)}, s32[4,2]{0,1:T(2,128)S(1)}, f32[4,128,128]{2,1,0:T(8,128)}, s32[]{:T(128)}) while((s32[]{:T(128)}, f32[512,512]{1,0:T(8,128)S(1)}, s32[4,2]{0,1:T(2,128)S(1)}, f32[4,128,128]{2,1,0:T(8,128)}, s32[]{:T(128)}) %tuple.34), condition=%wide.while_cond, body=%wide.while_body.sunk | while | flops 2 | bytes 132705 | solution.py:38
  376.9 0.6 fusion.64
  377.5 2.0 bitcast_dynamic-update-slice_fusion.2
  379.5 0.6 fusion.64
  380.1 2.0 bitcast_dynamic-update-slice_fusion.2
  382.2 0.6 fusion.64
  382.8 2.0 bitcast_dynamic-update-slice_fusion.2
  384.8 0.6 fusion.64
  385.4 2.0 bitcast_dynamic-update-slice_fusion.2
  387.4 40.1 %custom-call.34 = f32[4,128,128]{1,2,0:T(8,128)S(1)} custom-call(f32[4,128,128]{2,1,0:T(8,128)} %get-tuple-element.9), custom_call_target="InvertDiagBlocksLowerTriangular" | custom-call | tf_op jit(solution)/shard_map/jit(_solve_triangular)/triangular_solve | solution.py:38
  427.5 0.3 fusion.15
  427.8 0.4 convolution_subtract_fusion.2
  428.2 0.4 fusion.27
  428.7 0.4 convolution_subtract_fusion.1
  429.1 0.4 fusion.25
  429.5 0.6 convolution_subtract_fusion.3
  430.2 0.4 fusion.24
  430.7 0.3 copy.23
  431.0 1.6 gather_fusion
  432.7 9.0 %fusion.1 = f32[2048,512]{1,0:T(8,128)S(1)} fusion(f32[2048,512]{0,1:T(8,128)} %all-gather.8.cloned.1.call-done, f32[512,512]{1,0:T(8,128)S(1)} %gather_fusion, pred[512]{0:T(512)(128)(4,1)S(1)} %compare_and_fusion), kind=kOutput, calls=%fused_computation.18 | convolution fusion | flops 6442713088 | bytes 9437696 | tf_op jit(solution)/shard_map/dot_general | solution.py:46
  441.7 1.9 copy-done
  443.6 1.1 dynamic-slice_select_fusion
  444.8 1.6 constant_dynamic-slice_fusion.1
  446.3 1.0 copy.26
  447.3 61.8 %all-reduce.6.cloned.1.call-done = f32[512,512]{1,0:T(8,128)} async-done(((f32[512,512]{1,0:T(8,128)}), f32[512,512]{1,0:T(8,128)}) %all-reduce.6.cloned.1.call-update) | async-done | bytes 1048592 | tf_op jit(solution)/shard_map/psum | solution.py:12
  509.0 11.0 %convolution_subtract_fusion = f32[2048,512]{0,1:T(8,128)} fusion(f32[2048,512]{0,1:T(8,128)} %copy-done.1, f32[2048,512]{1,0:T(8,128)} %copy-done, f32[512,512]{1,0:T(8,128)} %all-reduce.6.cloned.1.call-done), kind=kOutput, calls=%fused_computation.4 | convolution fusion | flops 6443499520 | bytes 13631488 | tf_op jit(solution)/shard_map/dot_general | solution.py:55
  520.0 5.3 %copy.25 = f32[2048,512]{1,0:T(8,128)} copy(f32[2048,512]{0,1:T(8,128)} %convolution_subtract_fusion) | data formatting | bytes 8388608
  (33 shorter events, 0.9 us)
Async XLA Ops:
  7.2 81.3 %all-gather.6.cloned.1.call-start = ((), (), s32[]{:S(2)}) async-start(), calls=%async_computation | async-start | bytes 2162688 | tf_op jit(solution)/shard_map/all_gather | solution.py:24
  7.9 147.7 %all-reduce.4.cloned.1.call-start = ((), (), s32[]{:S(2)}) async-start(), calls=%async_computation.1 | async-start | bytes 1048576 | tf_op jit(solution)/shard_map/psum | solution.py:12
  90.4 65.2 %copy-start.2 = (bf16[512,2048]{0,1:T(8,128)(2,1)S(1)}, bf16[512,2048]{0,1:T(8,128)(2,1)}, u32[]{:S(2)}) copy-start(bf16[512,2048]{0,1:T(8,128)(2,1)} %all-gather.6.cloned.1.call-done) | copy-start | bytes 6291460
  90.4 177.3 %all-gather.10.cloned.1.call-start = ((), (), s32[]{:S(2)}) async-start(), calls=%async_computation.4 | async-start | bytes 2105344 | tf_op jit(solution)/shard_map/all_gather | solution.py:34
  159.3 2.0 copy-start.1
  161.9 270.8 %all-gather.8.cloned.1.call-start = ((), (), s32[]{:S(2)}) async-start(), calls=%async_computation.2 | async-start | bytes 4325376 | tf_op jit(solution)/shard_map/all_gather | solution.py:41
  163.5 345.5 %all-reduce.6.cloned.1.call-start = ((), (), s32[]{:S(2)}) async-start(), calls=%async_computation.3 | async-start | bytes 2097152 | tf_op jit(solution)/shard_map/psum | solution.py:12
  288.4 1.0 copy-start.3
  441.7 1.9 copy-start
Sparse Core Ops, SparseCore 0:
  10.6 77.8 all-gather.5
  90.8 64.7 all-reduce.3
  162.0 105.6 all-gather.9
  271.1 78.0 all-gather.7
  444.9 64.1 all-reduce.5
where the time goes:
time: 539 us; the launch traced here: 532 us
  waiting for transfers between devices  307 us (57%)
  other arithmetic  122 us (23%)
  local copies, waits for them, and re-layouts  53.5 us (10%)
  matrix products  32.1 us (6%)
  between operations  16.8 us (3%)
    psum x2, waiting for transfers between devices, from_root(): return lax.psum(jnp.where(mine, value, jnp.zeros_like(value)), axis)  121 us
    all_gather x1, waiting for transfers between devices, per_device(): diag_tiles = lax.all_gather(corner, ('row', 'col'), axis=0, tiled=True)  104 us
    all_gather x1, waiting for transfers between devices, per_device(): jac_rows = lax.all_gather(jacobian, 'col', axis=1, tiled=True)  80.5 us
    another operation x14, other arithmetic, per_device(): factor = jnp.linalg.cholesky(block)  78.6 us
    another operation x3, other arithmetic, per_device(): jax.scipy.linalg.solve_triangular(factor, jnp.eye(PW, dtype=jnp.float32),...  40.3 us
    unnamed x12, local copies, waits for them, and re-layouts  17.3 us
    dot_general x1, matrix products, per_device(): lax.dot_general(panel, far_rows, (((1,), (1,)), ((), ())), precision=lax....  11 us
  transfers between devices with their start and end apart: 5, of which 4 were waited for; matrix products, arithmetic and copies ran while one was open for 32% of the time, Pallas kernels for 0%

commit v1 on v0

v1 whole, which is shorter than its diff:
```python
import functools

import jax
import jax.numpy as jnp
from jax import lax
from jax.experimental import pallas as pl
from jax.experimental.pallas import tpu as pltpu
from jax.sharding import Mesh
from jax.sharding import PartitionSpec as P

PW = 512
NB = 16
T = 128
AXES = ("x", "core", "y", "z")
F32 = jnp.float32
BF16 = jnp.bfloat16
HI = lax.Precision.HIGHEST
VMEM = pltpu.VMEM


def nt(a, b, precision=None):
    return lax.dot_general(a, b, (((1,), (1,)), ((), ())), precision=precision, preferred_element_type=F32)


def nn(a, b, precision=None):
    return lax.dot_general(a, b, (((1,), (0,)), ((), ())), precision=precision, preferred_element_type=F32)


def tn(a, b):
    return lax.dot_general(a, b, (((0,), (0,)), ((), ())), preferred_element_type=F32)


def split(x):
    high = x.astype(BF16)
    return high, (x - high.astype(F32)).astype(BF16)


def prep_kernel(cols_ref, rows_ref, jac_ref, wide_ref, corner_ref, near_ref):
    cols = cols_ref[...].T[:NB]
    high, low = split(cols)
    for q in range(4):
        wide_ref[q] = high[:, q * PW : (q + 1) * PW]
        wide_ref[4 + q] = low[:, q * PW : (q + 1) * PW]
        wide_ref[8 + q] = jac_ref[q * NB : (q + 1) * NB, :]
    corner = jnp.concatenate([cols[:8, :64], cols[8:, :64]], axis=1)
    first, rest = split(corner)
    rest = corner - first.astype(F32)
    second = rest.astype(BF16)
    third = (rest - second.astype(F32)).astype(BF16)
    corner_ref[:, :T] = jnp.concatenate([first.astype(F32), second.astype(F32)], axis=0).astype(BF16)
    corner_ref[:, T:] = jnp.concatenate([third.astype(F32), jnp.zeros((8, T), F32)], axis=0).astype(BF16)
    high, low = split(rows_ref[...])
    for i in range(4):
        near_ref[i, :, :PW] = high[i * NB : (i + 1) * NB]
        near_ref[i, :, PW:] = low[i * NB : (i + 1) * NB]


def prep(normal, jac_t):
    rows = normal.shape[0]
    whole = pl.BlockSpec(memory_space=VMEM)
    return pl.pallas_call(
        prep_kernel,
        grid=(1,),
        in_specs=[
            pl.BlockSpec((rows, T), lambda i: (0, 0)),
            pl.BlockSpec((64, PW), lambda i: (0, 0)),
            pl.BlockSpec((64, PW), lambda i: (0, 0)),
        ],
        out_specs=[
            pl.BlockSpec((12, NB, PW), lambda i: (0, 0, 0)),
            pl.BlockSpec((NB, 2 * T), lambda i: (0, 0)),
            pl.BlockSpec((4, NB, 2 * PW), lambda i: (0, 0, 0)),
        ],
        out_shape=[
            jax.ShapeDtypeStruct((12, NB, PW), BF16),
            jax.ShapeDtypeStruct((NB, 2 * T), BF16),
            jax.ShapeDtypeStruct((4, NB, 2 * PW), BF16),
        ],
        compiler_params=pltpu.CompilerParams(vmem_limit_bytes=24 << 20),
    )(normal, normal, jac_t)


def factor_tile(tile):
    q = 8
    groups = T // q
    rows = [tile[q * i : q * (i + 1), :] for i in range(groups)]
    lane = lax.broadcasted_iota(jnp.int32, (q, T), 1)
    out = []
    spread = lambda v: jnp.broadcast_to(v, (q, T))
    for g in range(groups):
        base = g * q
        cols = {i: [spread(rows[i][:, base + l : base + l + 1]) for l in range(q)] for i in range(g, groups)}
        low = [[None] * q for _ in range(q)]
        inv = [[None] * q for _ in range(q)]
        pivot = [[spread(cols[g][l][k : k + 1, :]) if k >= l else None for l in range(q)] for k in range(q)]
        for j in range(q):
            d = pivot[j][j]
            for m in range(j):
                d = d - low[j][m] * low[j][m]
            r = lax.rsqrt(d)
            inv[j][j] = r
            for i in range(j + 1, q):
                t = pivot[i][j]
                for m in range(j):
                    t = t - low[i][m] * low[j][m]
                low[i][j] = t * r
        for i in range(q):
            for j in range(i):
                t = low[i][j] * inv[j][j]
                for m in range(j + 1, i):
                    t = t + low[i][m] * inv[m][j]
                inv[i][j] = -(t * inv[i][i])
        inside = (lane >= base) & (lane < base + q)
        top = [
            jnp.where(inside, jnp.where(lane == base + l, 1.0, 0.0), spread(rows[g][l : l + 1, :])) for l in range(q)
        ]
        done = []
        for k in range(q):
            t = inv[k][0] * top[0]
            for l in range(1, k + 1):
                t = t + inv[k][l] * top[l]
            done.append(t)
        weight = []
        for k in range(q):
            t = inv[k][k] * done[k]
            for l in range(k + 1, q):
                t = t + inv[l][k] * done[l]
            weight.append(t)
        sub = lax.broadcasted_iota(jnp.int32, (q, T), 0)
        mine = done[0]
        for k in range(1, q):
            mine = jnp.where(sub >= k, done[k], mine)
        out.append(jnp.where(lane < base + q, mine, 0.0))
        for i in range(g + 1, groups):
            acc = cols[i][0] * weight[0]
            for k in range(1, q):
                acc = acc + cols[i][k] * weight[k]
            rows[i] = jnp.where(inside, 0.0, rows[i]) - acc
    return jnp.concatenate(out, 0)


def factor(work, inv):
    inv[...] = jnp.zeros_like(inv)
    tiles = PW // T
    for b in range(tiles):
        lo, hi = b * T, (b + 1) * T
        here = factor_tile(work[lo:hi, lo:hi])
        inv[lo:hi, lo:hi] = here
        if b:
            inv[lo:hi, :lo] = nn(here, inv[lo:hi, :lo], HI)
        if b < tiles - 1:
            below = nt(work[hi:, lo:hi], here, HI)
            work[hi : hi + T, hi : hi + T] -= nt(below[:T], below[:T], HI)
            if b < tiles - 2:
                work[hi + T :, hi:] -= nt(below[T:], below, HI)
            inv[hi:, :hi] -= nn(below, inv[lo:hi, :hi], HI)


def block_kernel(
    core_ref, own_ref, other_ref, inv_hi, inv_lo, far_hi, far_lo, jac_first, jac_cols, work, inv, gram, pieces, thirds
):
    core = core_ref[0]
    for x in range(4):
        for ref, r in ((own_ref, 2 * x + core), (other_ref, 2 * x + 1 - core)):
            for a in range(4):
                at = pl.ds(pl.multiple_of(a * T + r * NB, NB), NB)
                jac_first[at, :] = ref[x, a, :, :PW]
                jac_cols[at, :] = ref[x, a, :, 5 * PW : 6 * PW]
                gram[at, :] = ref[x, a, :, 6 * PW : 7 * PW].astype(F32) + ref[x, a, :, 7 * PW :].astype(F32)
                for z in range(8):
                    row = (a * 8 + z) * NB
                    lanes = pl.ds(pl.multiple_of(r * T, T), T)
                    start = PW + z * 2 * T
                    pieces[row : row + NB, lanes] = ref[x, a, :, start : start + T]
                    thirds[row : row + NB, lanes] = ref[x, a, :, start + T : start + 2 * T]
    src = lax.broadcasted_iota(jnp.int32, (8 * T, PW), 0)
    dst = lax.broadcasted_iota(jnp.int32, (8 * T, PW), 1)
    to = (src // 16 % 4) * T + (src // T) * NB + src % NB
    for half in range(2):
        place = jnp.where((to == dst) & (src // 64 % 2 == half), 1.0, 0.0).astype(BF16)
        a = nn(pieces[...], place).reshape(32, 2, 8, PW)
        b = nn(thirds[...], place).reshape(32, 2, 8, PW)
        work.reshape(32, 2, 8, PW)[:, half] = a[:, 0] + a[:, 1] + b[:, 0]
    first = jac_first[...]
    work[...] += nt(first, first)
    gram[...] += nt(first, jac_cols[...])
    factor(work, inv)
    high, low = split(inv[...])
    inv_hi[...] = high
    inv_lo[...] = low
    high, low = split(nn(inv[...], gram[...], HI))
    far_hi[...] = high
    far_lo[...] = low


def block(core, own, other):
    whole = pl.BlockSpec(memory_space=VMEM)
    return pl.pallas_call(
        block_kernel,
        in_specs=[pl.BlockSpec(memory_space=pltpu.SMEM), whole, whole],
        out_specs=[whole] * 6,
        out_shape=[jax.ShapeDtypeStruct((PW, PW), BF16)] * 6,
        scratch_shapes=[
            VMEM((PW, PW), F32),
            VMEM((PW, PW), F32),
            VMEM((PW, PW), F32),
            VMEM((PW, 8 * T), BF16),
            VMEM((PW, 8 * T), BF16),
        ],
        compiler_params=pltpu.CompilerParams(vmem_limit_bytes=40 << 20),
    )(core, own, other)


def last_kernel(
    col_ref, normal_ref, high_ref, low_ref, jac_ref, inv_hi, inv_lo, far_hi, far_lo, first, cols, out_ref, panel_ref, save
):
    rows = jac_ref[...].reshape(PW, PW)
    panel_in = high_ref[...].reshape(PW, PW).astype(F32) + low_ref[...].reshape(PW, PW).astype(F32)
    panel_in = panel_in + nt(first[...], rows)
    high, low = split(panel_in)
    panel = nn(inv_hi[...], high) + (nn(inv_lo[...], high) + nn(inv_hi[...], low))
    save[...] = panel
    panel_ref[...] = save[pl.ds(pl.multiple_of(col_ref[0] * NB, NB), NB), :]
    high, low = split(panel)
    drop = tn(high, far_hi[...]) + (tn(low, far_hi[...]) + tn(high, far_lo[...]))
    out_ref[...] = normal_ref[...] + nt(rows, cols[...]) - drop


def last(col, normal, wide, inv_hi, inv_lo, far_hi, far_lo, first, cols):
    rows = normal.shape[0]
    whole = pl.BlockSpec((PW, PW), lambda q: (0, 0))
    return pl.pallas_call(
        last_kernel,
        grid=(rows // PW,),
        in_specs=[
            pl.BlockSpec(memory_space=pltpu.SMEM),
            pl.BlockSpec((PW, PW), lambda q: (q, 0)),
            pl.BlockSpec((32, 1, NB, PW), lambda q: (0, q, 0, 0)),
            pl.BlockSpec((32, 1, NB, PW), lambda q: (0, 4 + q, 0, 0)),
            pl.BlockSpec((8, 4, NB, PW), lambda q: (q, 2, 0, 0)),
        ]
        + [whole] * 6,
        out_specs=[
            pl.BlockSpec((PW, PW), lambda q: (q, 0)),
            pl.BlockSpec((NB, PW), lambda q: (0, q)),
        ],
        out_shape=[
            jax.ShapeDtypeStruct((rows, PW), F32),
            jax.ShapeDtypeStruct((NB, rows), F32),
        ],
        scratch_shapes=[VMEM((PW, PW), F32)],
        compiler_params=pltpu.CompilerParams(vmem_limit_bytes=40 << 20),
    )(col, normal, wide, wide, wide, inv_hi, inv_lo, far_hi, far_lo, first, cols)


def position(r, y, z):
    return (r * 4 + y) * 8 + z


def spread_over(value, axis, count):
    return lax.all_to_all(jnp.broadcast_to(value[None], (count,) + value.shape), axis, 0, 0, tiled=True)


def per_device(normal, jacobian):
    core = lax.axis_index("core").astype(jnp.int32)[None]
    col = (lax.axis_index("y") * 8 + lax.axis_index("z")).astype(jnp.int32)[None]
    jac_t = jacobian.T
    wide, corner, near = prep(normal, jac_t)
    wide = lax.all_gather(wide, ("y", "z"), axis=0, tiled=False)
    tiles = lax.all_to_all(jac_t.reshape(4, NB, PW), "y", 0, 0, tiled=True)
    swap = [(position(r, y, z), position(z, y, r)) for r in range(8) for y in range(4) for z in range(8)]
    swapped = lax.ppermute(tiles, AXES, swap)
    got = spread_over(jnp.concatenate([tiles[0], corner], axis=1), "z", 8)
    sent = jnp.concatenate([got[0, :, :PW]] + [got[z, :, PW:] for z in range(8)], axis=1)
    got = spread_over(sent, "y", 4)
    sent = jnp.concatenate([got, swapped, near], axis=2)
    own = spread_over(sent, "x", 4)
    flip = [(position(r, y, z), position(r ^ 1, y, z)) for r in range(8) for y in range(4) for z in range(8)]
    other = lax.ppermute(own, AXES, flip)
    parts = block(core, own, other)
    updated, panel_t = last(col, normal, wide, *parts)
    return updated, panel_t.T


def solution(mesh):
    fine = Mesh(mesh.devices.reshape(4, 2, 4, 8), AXES)
    rows, cols = ("x", "core"), ("y", "z")
    return jax.shard_map(
        per_device,
        mesh=fine,
        in_specs=(P(rows, cols), P(None, AXES)),
        out_specs=(P(rows, cols), P(rows, cols)),
        check_vma=False,
    )
```

time: 539 us -> 150 us (0.28); the launches traced: 532 us -> 150 us
  waiting for transfers between devices: 307 us -> 6.93 us
  other arithmetic: 122 us -> 0.04 us
  blocking collectives: 0 us -> 52.9 us
  Pallas kernels: 0 us -> 42.8 us
  local copies, waits for them, and re-layouts: 53.5 us -> 16.4 us
  matrix products: 32.1 us -> 0 us
  starting transfers between devices: 0.2 us -> 16.6 us
    all_gather x3 -> x1, waiting for transfers between devices: 184 us -> 0.01 us  [per_device(): wide = lax.all_gather(wide, ('y', 'z'), axis=0, tiled=False)]
    psum x2 -> x0, waiting for transfers between devices: 121 us -> none  [from_root(): return lax.psum(jnp.where(mine, value, jnp.zeros_like(value)), axis)]
    another operation x17 -> x0, other arithmetic: 119 us -> none  [the longest x14 78.6 us: per_device(): factor = jnp.linalg.cholesky(block)]
    all_to_all x0 -> x3, blocking collectives: none -> 52.9 us  [the longest x2 43.6 us: spread_over(): lax.all_to_all(jnp.broadcast_to(value[None], (count,) + value.shape), axi...]
    pallas_call x0 -> x3, Pallas kernels: none -> 42.8 us  [the longest x1 30 us: block(): pl.pallas_call(block_kernel, in_specs=[pl.BlockSpec(memory_space=pltpu.SM...]
    dot_general x3 -> x0, matrix products: 23.7 us -> none  [the longest x1 11 us: per_device(): lax.dot_general(panel, far_rows, (((1,), (1,)), ((), ())), precision=lax....]
    ppermute x0 -> x2, starting transfers between devices: none -> 13.1 us  [the longest x1 6.68 us: per_device(): other = lax.ppermute(own, AXES, flip)]
    another operation x17 -> x0, local copies, waits for them, and re-layouts: 10.7 us -> none
  transfers between devices with their start and end apart: 5 -> 4, of which waited for: 4 -> 2; matrix products, arithmetic and copies ran while one was open for 32% -> 1% of each run, Pallas kernels for 0% -> 20%
where the time goes in v1:
time: 150 us
  blocking collectives  52.9 us (35%)
  Pallas kernels  42.8 us (29%)
  starting transfers between devices  16.6 us (11%)
  local copies, waits for them, and re-layouts  16.4 us (11%)
  between operations  14.2 us (9%)
  waiting for transfers between devices  6.93 us (5%)
    all_to_all x2, blocking collectives, spread_over(): lax.all_to_all(jnp.broadcast_to(value[None], (count,) + value.shape), axi...  43.6 us
    pallas_call x1, Pallas kernels, block(): pl.pallas_call(block_kernel, in_specs=[pl.BlockSpec(memory_space=pltpu.SM...  30 us
    unnamed x34, local copies, waits for them, and re-layouts  15.3 us
    pallas_call x1, Pallas kernels, last(): pl.pallas_call(last_kernel, grid=(rows // PW,), in_specs=[pl.BlockSpec(me...  11.7 us
    all_to_all x1, blocking collectives, per_device(): tiles = lax.all_to_all(jac_t.reshape(4, NB, PW), 'y', 0, 0, tiled=True)  9.29 us
    ppermute x1, starting transfers between devices, per_device(): other = lax.ppermute(own, AXES, flip)  6.68 us
    ppermute x1, starting transfers between devices, per_device(): swapped = lax.ppermute(tiles, AXES, swap)  6.44 us
    ppermute x1, waiting for transfers between devices, per_device(): other = lax.ppermute(own, AXES, flip)  3.92 us
  transfers between devices with their start and end apart: 4, of which 2 were waited for; matrix products, arithmetic and copies ran while one was open for 1% of the time, Pallas kernels for 20%

profile of v1, /device:TPU:1, one launch (start us, length us, event | category | flops | bytes accessed | tf_op | source)
XLA Modules:
  0.0 149.8 jit_solution(16676070260521618151)
XLA Ops:
  7.2 0.0 all-gather.3.cloned.1.call-start
  7.2 0.0 copy-start.1
  7.2 2.2 %copy-done.1 = f32[2048,512]{1,0:T(8,128)S(1)} copy-done((f32[2048,512]{1,0:T(8,128)S(1)}, f32[2048,512]{1,0:T(8,128)}, u32[]{:S(2)}) %copy-start.1) | copy-done | bytes 4194328
  9.4 0.0 copy-start.11
  9.4 0.8 copy-done.11
  10.2 0.0 copy-start.12
  10.2 1.0 shard_map.41
  11.3 0.0 all-gather.3.cloned.1.call-update
  11.3 0.0 copy-done.12
  11.3 9.3 %all_to_all.20 = bf16[4,16,512]{2,1,0:T(8,128)(2,1)S(1)} all-to-all(bf16[4,16,512]{2,1,0:T(8,128)(2,1)S(1)} %bitcast.49), channel_id=1, replica_groups=mesh['x'=4,'core'=2,'y'=4,'z'=8] {'y'}, dimensions={0} | all-to-all | bytes 131072 | tf_op jit(solution)/shard_map/all_to_all | solution.py:270
  20.6 17.2 %all_to_all.21 = bf16[8,16,768]{2,1,0:T(8,128)(2,1)S(1)} all-to-all(bf16[8,16,768]{2,1,0:T(8,128)(2,1)S(1)} %broadcast_in_dim.12), channel_id=1, replica_groups=mesh['x'=4,'core'=2,'y'=4,'z'=8] {'z'}, dimensions={0} | all-to-all | bytes 393216 | tf_op jit(solution)/shard_map/all_to_all | solution.py:261
  37.9 0.7 broadcast_in_dim.13
  38.6 3.5 %all-to-all-start.2 = ((bf16[4,16,2560]{2,1,0:T(8,128)(2,1)}), bf16[4,16,2560]{2,1,0:T(8,128)(2,1)S(1)}, u32[]{:S(2)}, u32[]{:S(2)}) async-start(bf16[4,16,2560]{2,1,0:T(8,128)(2,1)} %broadcast_in_dim.13), calls=%async_computation.2 | async-start | bytes 655360 | tf_op jit(solution)/shard_map/all_to_all | solution.py:261
  42.1 6.4 %collective-permute-start = (bf16[4,16,512]{2,1,0:T(8,128)(2,1)S(1)}, bf16[4,16,512]{2,1,0:T(8,128)(2,1)S(1)}, u32[]{:S(2)}, u32[]{:S(2)}) collective-permute-start(bf16[4,16,512]{2,1,0:T(8,128)(2,1)S(1)} %all_to_all.20), channel_id=1, source_target_pairs={{0,0},{1,32},{2,64},{3,96},{4,128},{5,160},{6,192},{7,224},{8,8},{... | collective-permute-start | bytes 196616 | tf_op jit(solution)/shard_map/ppermute | solution.py:272
  48.5 3.0 %collective-permute-done = bf16[4,16,512]{2,1,0:T(8,128)(2,1)S(1)} collective-permute-done((bf16[4,16,512]{2,1,0:T(8,128)(2,1)S(1)}, bf16[4,16,512]{2,1,0:T(8,128)(2,1)S(1)}, u32[]{:S(2)}, u32[]{:S(2)}) %collective-permute-start) | collective-permute-done | bytes 65568 | tf_op jit(solution)/shard_map/ppermute | solution.py:272
  51.5 0.0 all-to-all-done.2
  51.6 0.2 broadcast_in_dim.28
  51.8 26.5 %all_to_all.22.own_ref = bf16[4,4,16,4096]{3,2,1,0:T(8,128)(2,1)S(1)} all-to-all(bf16[4,4,16,4096]{3,2,1,0:T(8,128)(2,1)S(1)} %broadcast_in_dim.28), channel_id=1, replica_groups=mesh['x'=4,'core'=2,'y'=4,'z'=8] {'x'}, dimensions={0} | all-to-all | bytes 4194304 | tf_op jit(solution)/shard_map/all_to_all | solution.py:261
  78.3 6.7 %collective-permute-start.1 = (bf16[4,4,16,4096]{3,2,1,0:T(8,128)(2,1)S(1)}, bf16[4,4,16,4096]{3,2,1,0:T(8,128)(2,1)}, u32[]{:S(2)}, u32[]{:S(2)}) collective-permute-start(bf16[4,4,16,4096]{3,2,1,0:T(8,128)(2,1)S(1)} %all_to_all.22.own_ref), channel_id=1, source_target_pairs={{0,32},{1,33},{2,34},{3,35},{4,36},{5,37},{6,38},{7,39},{8,40},{9,... | collective-permute-start | bytes 6291464 | tf_op jit(solution)/shard_map/ppermute | solution.py:279
  84.9 3.9 %collective-permute-done.1.other_ref = bf16[4,4,16,4096]{3,2,1,0:T(8,128)(2,1)} collective-permute-done((bf16[4,4,16,4096]{3,2,1,0:T(8,128)(2,1)S(1)}, bf16[4,4,16,4096]{3,2,1,0:T(8,128)(2,1)}, u32[]{:S(2)}, u32[]{:S(2)}) %collective-permute-start.1) | collective-permute-done | bytes 2097184 | tf_op jit(solution)/shard_map/ppermute | solution.py:279
  88.9 30.0 %shard_map.42 = (bf16[512,512]{1,0:T(8,128)(2,1)S(1)}, bf16[512,512]{1,0:T(8,128)(2,1)S(1)}, bf16[512,512]{1,0:T(8,128)(2,1)S(1)}, bf16[512,512]{1,0:T(8,128)(2,...) custom-call(s32[1]{0:T(128)} %bitcast.3.core_ref, bf16[4,4,16,4096]{3,2,1,0:T(8,128)(2,1)S(1)} %all_to_all.22.own_ref, ...), custom_call_target="tpu_custom_call" | custom-call | tf_op jit(solution)/shard_map/pallas_call | solution.py:198
  118.9 0.0 copy-start.3
  118.9 0.8 copy-done.3
  119.6 0.0 copy-start.5
  119.7 0.8 copy-done.5
  120.4 0.0 copy-start.7
  120.4 0.8 copy-done.7
  121.2 0.0 copy-start.9
  121.2 0.8 copy-done.9
  122.0 0.0 all-gather.3.cloned.1.call-done
  122.0 0.0 copy-start
  122.0 2.8 %copy-done = bf16[384,16,512]{2,1,0:T(8,128)(2,1)S(1)} copy-done((bf16[384,16,512]{2,1,0:T(8,128)(2,1)S(1)}, bf16[384,16,512]{2,1,0:T(8,128)(2,1)}, u32[]{:S(2)}) %copy-start) | copy-done | bytes 6291480
  124.8 0.0 copy-start.2
  124.8 2.2 %copy-done.2 = f32[2048,512]{1,0:T(8,128)S(1)} copy-done((f32[2048,512]{1,0:T(8,128)S(1)}, f32[2048,512]{1,0:T(8,128)}, u32[]{:S(2)}) %copy-start.2) | copy-done | bytes 4194328
  127.0 0.0 copy-start.4
  127.0 1.0 copy-done.4
  128.0 0.0 copy-start.6
  128.1 1.0 copy-done.6
  129.1 0.0 copy-start.8
  129.1 1.0 copy-done.8
  130.1 0.0 copy-start.10
  130.1 1.0 copy-done.10
  131.2 11.7 %shard_map.43 = (f32[2048,512]{1,0:T(8,128)}, f32[16,2048]{1,0:T(8,128)}) custom-call(s32[1]{0:T(128)} %bitcast.col_ref, f32[2048,512]{1,0:T(8,128)S(1)} %copy-done.2, bf16[32,12,16,512]{3,2,1,0:T(8,128)(2,1)S(1)} %bitcast.45, bf16[32,12,16,512]{3,2,1,0:T(8,128)(2,1)S(1)} %bitcast.46, bf16[32,12,16,512]{3,2,1,0:T(8,128)(2,1)S(1)} %bitcast.47, ...), custom_call_target="tpu_custom_call" | custom-call | tf_op jit(solution)/shard_map/pallas_call | solution.py:232
  (13 shorter events, 0.1 us)
Async XLA Ops:
  7.2 114.9 %all-gather.3.cloned.1.call-start = ((), (), s32[]{:S(2)}) async-start(), calls=%async_computation.4 | async-start | bytes 6488064 | tf_op jit(solution)/shard_map/all_gather | solution.py:269
  7.2 2.2 %copy-start.1 = (f32[2048,512]{1,0:T(8,128)S(1)}, f32[2048,512]{1,0:T(8,128)}, u32[]{:S(2)}) copy-start(f32[2048,512]{1,0:T(8,128)} %normal_ref.1) | copy-start | bytes 12582916
  9.4 0.8 copy-start.11
  10.2 1.1 copy-start.12
  38.6 12.9 %all-to-all-start.2 = ((bf16[4,16,2560]{2,1,0:T(8,128)(2,1)}), bf16[4,16,2560]{2,1,0:T(8,128)(2,1)S(1)}, u32[]{:S(2)}, u32[]{:S(2)}) async-start(bf16[4,16,2560]{2,1,0:T(8,128)(2,1)} %broadcast_in_dim.13), calls=%async_computation.2 | async-start | bytes 655360 | tf_op jit(solution)/shard_map/all_to_all | solution.py:261
  42.1 9.4 %collective-permute-start = (bf16[4,16,512]{2,1,0:T(8,128)(2,1)S(1)}, bf16[4,16,512]{2,1,0:T(8,128)(2,1)S(1)}, u32[]{:S(2)}, u32[]{:S(2)}) collective-permute-start(bf16[4,16,512]{2,1,0:T(8,128)(2,1)S(1)} %all_to_all.20), channel_id=1, source_target_pairs={{0,0},{1,32},{2,64},{3,96},{4,128},{5,160},{6,192},{7,224},{8,8},{... | collective-permute-start | bytes 196616 | tf_op jit(solution)/shard_map/ppermute | solution.py:272
  78.3 10.6 %collective-permute-start.1 = (bf16[4,4,16,4096]{3,2,1,0:T(8,128)(2,1)S(1)}, bf16[4,4,16,4096]{3,2,1,0:T(8,128)(2,1)}, u32[]{:S(2)}, u32[]{:S(2)}) collective-permute-start(bf16[4,4,16,4096]{3,2,1,0:T(8,128)(2,1)S(1)} %all_to_all.22.own_ref), channel_id=1, source_target_pairs={{0,32},{1,33},{2,34},{3,35},{4,36},{5,37},{6,38},{7,39},{8,40},{9,... | collective-permute-start | bytes 6291464 | tf_op jit(solution)/shard_map/ppermute | solution.py:279
  118.9 0.8 copy-start.3
  119.6 0.8 copy-start.5
  120.4 0.8 copy-start.7
  121.2 0.8 copy-start.9
  122.0 2.8 %copy-start = (bf16[384,16,512]{2,1,0:T(8,128)(2,1)S(1)}, bf16[384,16,512]{2,1,0:T(8,128)(2,1)}, u32[]{:S(2)}) copy-start(bf16[384,16,512]{2,1,0:T(8,128)(2,1)} %all-gather.3.cloned.1.call-done) | copy-start | bytes 18874372
  124.8 2.2 %copy-start.2 = (f32[2048,512]{1,0:T(8,128)S(1)}, f32[2048,512]{1,0:T(8,128)}, u32[]{:S(2)}) copy-start(f32[2048,512]{1,0:T(8,128)} %normal_ref.1) | copy-start | bytes 12582916
  127.0 1.0 copy-start.4
  128.0 1.0 copy-start.6
  129.1 1.0 copy-start.8
  130.1 1.0 copy-start.10
Sparse Core Ops, SparseCore 0:
  11.4 93.2 all-gather.2

commit v2 on v1

--- a/solution.py
+++ b/solution.py
@@ -42,13 +42,7 @@
         wide_ref[q] = high[:, q * PW : (q + 1) * PW]
         wide_ref[4 + q] = low[:, q * PW : (q + 1) * PW]
         wide_ref[8 + q] = jac_ref[q * NB : (q + 1) * NB, :]
-    corner = jnp.concatenate([cols[:8, :64], cols[8:, :64]], axis=1)
-    first, rest = split(corner)
-    rest = corner - first.astype(F32)
-    second = rest.astype(BF16)
-    third = (rest - second.astype(F32)).astype(BF16)
-    corner_ref[:, :T] = jnp.concatenate([first.astype(F32), second.astype(F32)], axis=0).astype(BF16)
-    corner_ref[:, T:] = jnp.concatenate([third.astype(F32), jnp.zeros((8, T), F32)], axis=0).astype(BF16)
+    corner_ref[...] = jnp.concatenate([cols[:8, :64], cols[8:, :64]], axis=1)
     high, low = split(rows_ref[...])
     for i in range(4):
         near_ref[i, :, :PW] = high[i * NB : (i + 1) * NB]
@@ -57,7 +51,6 @@
 
 def prep(normal, jac_t):
     rows = normal.shape[0]
-    whole = pl.BlockSpec(memory_space=VMEM)
     return pl.pallas_call(
         prep_kernel,
         grid=(1,),
@@ -68,15 +61,15 @@
         ],
         out_specs=[
             pl.BlockSpec((12, NB, PW), lambda i: (0, 0, 0)),
-            pl.BlockSpec((NB, 2 * T), lambda i: (0, 0)),
+            pl.BlockSpec((8, T), lambda i: (0, 0)),
             pl.BlockSpec((4, NB, 2 * PW), lambda i: (0, 0, 0)),
         ],
         out_shape=[
             jax.ShapeDtypeStruct((12, NB, PW), BF16),
-            jax.ShapeDtypeStruct((NB, 2 * T), BF16),
+            jax.ShapeDtypeStruct((8, T), F32),
             jax.ShapeDtypeStruct((4, NB, 2 * PW), BF16),
         ],
-        compiler_params=pltpu.CompilerParams(vmem_limit_bytes=24 << 20),
+        compiler_params=pltpu.CompilerParams(vmem_limit_bytes=62 << 20),
     )(normal, normal, jac_t)
 
 
@@ -156,41 +149,42 @@
             inv[hi:, :hi] -= nn(below, inv[lo:hi, :hi], HI)
 
 
-def block_kernel(
-    core_ref, own_ref, other_ref, inv_hi, inv_lo, far_hi, far_lo, jac_first, jac_cols, work, inv, gram, pieces, thirds
-):
+def place(refs, core, store):
+    for x in range(4):
+        for ref, r in ((refs[0], 2 * x + core), (refs[1], 2 * x + 1 - core)):
+            for a in range(4):
+                store(ref, x, a, r)
+
+
+def tile_rows(a, r):
+    return pl.ds(pl.multiple_of(a * T + r * NB, NB), NB)
+
+
+def block_kernel(core_ref, own_ref, other_ref, inv_ref, first_ref, work, pieces):
     core = core_ref[0]
-    for x in range(4):
-        for ref, r in ((own_ref, 2 * x + core), (other_ref, 2 * x + 1 - core)):
-            for a in range(4):
-                at = pl.ds(pl.multiple_of(a * T + r * NB, NB), NB)
-                jac_first[at, :] = ref[x, a, :, :PW]
-                jac_cols[at, :] = ref[x, a, :, 5 * PW : 6 * PW]
-                gram[at, :] = ref[x, a, :, 6 * PW : 7 * PW].astype(F32) + ref[x, a, :, 7 * PW :].astype(F32)
-                for z in range(8):
-                    row = (a * 8 + z) * NB
-                    lanes = pl.ds(pl.multiple_of(r * T, T), T)
-                    start = PW + z * 2 * T
-                    pieces[row : row + NB, lanes] = ref[x, a, :, start : start + T]
-                    thirds[row : row + NB, lanes] = ref[x, a, :, start + T : start + 2 * T]
+
+    def store(ref, x, a, r):
+        upper, lower = ref[x, a, :, :PW], ref[x, a, :, PW : 2 * PW]
+        first_ref[tile_rows(a, r), :] = jnp.concatenate([upper, lower], axis=0).astype(BF16)
+        lanes = pl.ds(pl.multiple_of(r * T, T), T)
+        for z in range(8):
+            start = 2 * PW + z * T
+            pieces[(a * 8 + z) * 8 : (a * 8 + z + 1) * 8, lanes] = ref[x, a, :, start : start + T]
+
+    place((own_ref, other_ref), core, store)
     src = lax.broadcasted_iota(jnp.int32, (8 * T, PW), 0)
     dst = lax.broadcasted_iota(jnp.int32, (8 * T, PW), 1)
     to = (src // 16 % 4) * T + (src // T) * NB + src % NB
+    high, rest = split(pieces[...])
+    rest = pieces[...] - high.astype(F32)
+    middle, low = split(rest)
     for half in range(2):
-        place = jnp.where((to == dst) & (src // 64 % 2 == half), 1.0, 0.0).astype(BF16)
-        a = nn(pieces[...], place).reshape(32, 2, 8, PW)
-        b = nn(thirds[...], place).reshape(32, 2, 8, PW)
-        work.reshape(32, 2, 8, PW)[:, half] = a[:, 0] + a[:, 1] + b[:, 0]
-    first = jac_first[...]
+        move = jnp.where((to == dst) & (src // 64 % 2 == half), 1.0, 0.0).astype(BF16)
+        part = nn(high, move) + nn(middle, move) + nn(low, move)
+        work.reshape(32, 2, 8, PW)[:, half] = part.reshape(32, 8, PW)
+    first = first_ref[...]
     work[...] += nt(first, first)
-    gram[...] += nt(first, jac_cols[...])
-    factor(work, inv)
-    high, low = split(inv[...])
-    inv_hi[...] = high
-    inv_lo[...] = low
-    high, low = split(nn(inv[...], gram[...], HI))
-    far_hi[...] = high
-    far_lo[...] = low
+    factor(work, inv_ref)
 
 
 def block(core, own, other):
@@ -198,17 +192,41 @@
     return pl.pallas_call(
         block_kernel,
         in_specs=[pl.BlockSpec(memory_space=pltpu.SMEM), whole, whole],
-        out_specs=[whole] * 6,
-        out_shape=[jax.ShapeDtypeStruct((PW, PW), BF16)] * 6,
-        scratch_shapes=[
-            VMEM((PW, PW), F32),
-            VMEM((PW, PW), F32),
-            VMEM((PW, PW), F32),
-            VMEM((PW, 8 * T), BF16),
-            VMEM((PW, 8 * T), BF16),
-        ],
-        compiler_params=pltpu.CompilerParams(vmem_limit_bytes=40 << 20),
+        out_specs=[whole] * 2,
+        out_shape=[jax.ShapeDtypeStruct((PW, PW), F32), jax.ShapeDtypeStruct((PW, PW), BF16)],
+        scratch_shapes=[VMEM((PW, PW), F32), VMEM((256, 8 * T), F32)],
+        compiler_params=pltpu.CompilerParams(vmem_limit_bytes=62 << 20),
     )(core, own, other)
+
+
+def far_kernel(place_ref, inv_ref, first_ref, near0, near1, near2, near3, inv_hi, inv_lo, far_hi, far_lo, cols, gram):
+    core = place_ref[0]
+    for k, near in enumerate((near0, near1, near2, near3)):
+        x = lax.rem(place_ref[1] + 4 - k, 4)
+        for side in range(2):
+            r = 2 * x + (core if side == 0 else 1 - core)
+            for a in range(4):
+                at = tile_rows(a, r)
+                cols[at, :] = near[side, a, :, :PW]
+                gram[at, :] = near[side, a, :, PW : 2 * PW].astype(F32) + near[side, a, :, 2 * PW :].astype(F32)
+    high, low = split(inv_ref[...])
+    inv_hi[...] = high
+    inv_lo[...] = low
+    high, low = split(nn(inv_ref[...], gram[...] + nt(first_ref[...], cols[...]), HI))
+    far_hi[...] = high
+    far_lo[...] = low
+
+
+def far(where, inv, first, near):
+    whole = pl.BlockSpec(memory_space=VMEM)
+    return pl.pallas_call(
+        far_kernel,
+        in_specs=[pl.BlockSpec(memory_space=pltpu.SMEM)] + [whole] * 6,
+        out_specs=[whole] * 5,
+        out_shape=[jax.ShapeDtypeStruct((PW, PW), BF16)] * 5,
+        scratch_shapes=[VMEM((PW, PW), F32)],
+        compiler_params=pltpu.CompilerParams(vmem_limit_bytes=62 << 20),
+    )(where, inv, first, *near)
 
 
 def last_kernel(
@@ -249,7 +267,7 @@
             jax.ShapeDtypeStruct((NB, rows), F32),
         ],
         scratch_shapes=[VMEM((PW, PW), F32)],
-        compiler_params=pltpu.CompilerParams(vmem_limit_bytes=40 << 20),
+        compiler_params=pltpu.CompilerParams(vmem_limit_bytes=62 << 20),
     )(col, normal, wide, wide, wide, inv_hi, inv_lo, far_hi, far_lo, first, cols)
 
 
@@ -261,24 +279,32 @@
     return lax.all_to_all(jnp.broadcast_to(value[None], (count,) + value.shape), axis, 0, 0, tiled=True)
 
 
+def moves(to):
+    return [(position(r, y, z), position(*to(r, y, z))) for r in range(8) for y in range(4) for z in range(8)]
+
+
 def per_device(normal, jacobian):
-    core = lax.axis_index("core").astype(jnp.int32)[None]
+    core, x = lax.axis_index("core").astype(jnp.int32), lax.axis_index("x").astype(jnp.int32)
+    where = jnp.stack([core, x])
     col = (lax.axis_index("y") * 8 + lax.axis_index("z")).astype(jnp.int32)[None]
     jac_t = jacobian.T
     wide, corner, near = prep(normal, jac_t)
     wide = lax.all_gather(wide, ("y", "z"), axis=0, tiled=False)
     tiles = lax.all_to_all(jac_t.reshape(4, NB, PW), "y", 0, 0, tiled=True)
-    swap = [(position(r, y, z), position(z, y, r)) for r in range(8) for y in range(4) for z in range(8)]
-    swapped = lax.ppermute(tiles, AXES, swap)
-    got = spread_over(jnp.concatenate([tiles[0], corner], axis=1), "z", 8)
-    sent = jnp.concatenate([got[0, :, :PW]] + [got[z, :, PW:] for z in range(8)], axis=1)
+    swapped = lax.ppermute(tiles, AXES, moves(lambda r, y, z: (z, y, r)))
+    flip = moves(lambda r, y, z: (r ^ 1, y, z))
+    near = jnp.concatenate([swapped, near], axis=2)
+    near = jnp.stack([near, lax.ppermute(near, AXES, flip)])
+    head = tiles[0].astype(F32)
+    got = spread_over(jnp.concatenate([head[:8], head[8:], corner], axis=1), "z", 8)
+    sent = jnp.concatenate([got[0, :, : 2 * PW]] + [got[z, :, 2 * PW :] for z in range(8)], axis=1)
     got = spread_over(sent, "y", 4)
-    sent = jnp.concatenate([got, swapped, near], axis=2)
-    own = spread_over(sent, "x", 4)
-    flip = [(position(r, y, z), position(r ^ 1, y, z)) for r in range(8) for y in range(4) for z in range(8)]
+    own = spread_over(got, "x", 4)
     other = lax.ppermute(own, AXES, flip)
-    parts = block(core, own, other)
-    updated, panel_t = last(col, normal, wide, *parts)
+    nears = [near] + [lax.ppermute(near, AXES, moves(lambda r, y, z: ((r + 2 * k) % 8, y, z))) for k in (1, 2, 3)]
+    inv, first = block(core[None], own, other)
+    inv_hi, inv_lo, far_hi, far_lo, cols = far(where, inv, first, nears)
+    updated, panel_t = last(col, normal, wide, inv_hi, inv_lo, far_hi, far_lo, first, cols)
     return updated, panel_t.T
 
 

time: 150 us -> 133 us (0.89)
  blocking collectives: 52.9 us -> 37.9 us
  local copies, waits for them, and re-layouts: 16.4 us -> 1.9 us
  Pallas kernels: 42.8 us -> 50.2 us
  starting transfers between devices: 16.6 us -> 20.8 us
    all_to_all x2, blocking collectives: 43.6 us -> 28.5 us  [spread_over(): lax.all_to_all(jnp.broadcast_to(value[None], (count,) + value.shape), axi...]
    unnamed x34 -> x19, local copies, waits for them, and re-layouts: 15.3 us -> 0.76 us
    pallas_call x0 -> x1, Pallas kernels: none -> 5.71 us  [far(): pl.pallas_call(far_kernel, in_specs=[pl.BlockSpec(memory_space=pltpu.SMEM...]
    ppermute x1 -> x5, starting transfers between devices: 6.44 us -> 10.8 us  [the longest x1 6.62 us: per_device(): swapped = lax.ppermute(tiles, AXES, moves(lambda r, y, z: (z, y, r)))]
    ppermute x1, waiting for transfers between devices: 3.92 us -> 0.01 us  [per_device(): other = lax.ppermute(own, AXES, flip)]
    all_to_all x1, waiting for transfers between devices: 0.01 us -> 3.52 us  [spread_over(): lax.all_to_all(jnp.broadcast_to(value[None], (count,) + value.shape), axi...]
    pallas_call x1, Pallas kernels: 11.7 us -> 14.1 us  [last(): pl.pallas_call(last_kernel, grid=(rows // PW,), in_specs=[pl.BlockSpec(me...]
    pallas_call x1, Pallas kernels: 30 us -> 28 us  [block(): pl.pallas_call(block_kernel, in_specs=[pl.BlockSpec(memory_space=pltpu.SM...]
  transfers between devices with their start and end apart: 4 -> 8, of which waited for: 2 -> 2; matrix products, arithmetic and copies ran while one was open for 1% -> 2% of each run, Pallas kernels for 20% -> 25%
where the time goes in v2:
time: 133 us; the launch traced here: 132 us
  Pallas kernels  50.2 us (38%)
  blocking collectives  37.9 us (28%)
  starting transfers between devices  20.8 us (16%)
  between operations  14.2 us (11%)
  waiting for transfers between devices  5.98 us (4%)
  local copies, waits for them, and re-layouts  1.9 us (1%)
  other arithmetic  1.38 us (1%)
    all_to_all x2, blocking collectives, spread_over(): lax.all_to_all(jnp.broadcast_to(value[None], (count,) + value.shape), axi...  28.5 us
    pallas_call x1, Pallas kernels, block(): pl.pallas_call(block_kernel, in_specs=[pl.BlockSpec(memory_space=pltpu.SM...  28 us
    pallas_call x1, Pallas kernels, last(): pl.pallas_call(last_kernel, grid=(rows // PW,), in_specs=[pl.BlockSpec(me...  14.1 us
    all_to_all x1, blocking collectives, per_device(): tiles = lax.all_to_all(jac_t.reshape(4, NB, PW), 'y', 0, 0, tiled=True)  9.42 us
    ppermute x1, starting transfers between devices, per_device(): swapped = lax.ppermute(tiles, AXES, moves(lambda r, y, z: (z, y, r)))  6.62 us
    ppermute x1, starting transfers between devices, per_device(): other = lax.ppermute(own, AXES, flip)  5.9 us
    pallas_call x1, Pallas kernels, far(): pl.pallas_call(far_kernel, in_specs=[pl.BlockSpec(memory_space=pltpu.SMEM...  5.71 us
    all_to_all x1, starting transfers between devices, spread_over(): lax.all_to_all(jnp.broadcast_to(value[None], (count,) + value.shape), axi...  4.12 us
  transfers between devices with their start and end apart: 8, of which 2 were waited for; matrix products, arithmetic and copies ran while one was open for 2% of the time, Pallas kernels for 25%

profile of v2, /device:TPU:1, one launch (start us, length us, event | category | flops | bytes accessed | tf_op | source)
XLA Modules:
  0.0 132.4 jit_solution(8588706706189284468)
XLA Ops:
  7.2 0.0 all-gather.3.cloned.1.call-start
  7.2 0.0 copy-start.3
  7.2 2.4 %shard_map.41 = (bf16[12,16,512]{2,1,0:T(8,128)(2,1)}, f32[8,128]{1,0:T(8,128)}, bf16[4,16,1024]{2,1,0:T(8,128)(2,1)}) custom-call(f32[2048,512]{1,0:T(8,128)} %normal_ref.1, f32[2048,512]{1,0:T(8,128)} %normal_ref.1, bf16[64,512]{1,0:T(8,128)(2,1)} %bitcast.54), custom_call_target="tpu_custom_call" | custom-call | tf_op jit(solution)/shard_map/pallas_call | solution.py:54
  9.6 0.0 copy-start.4
  9.6 0.0 all-gather.3.cloned.1.call-update
  9.6 0.0 copy-done.3
  9.6 9.4 %all_to_all.20 = bf16[4,16,512]{2,1,0:T(8,128)(2,1)S(1)} all-to-all(bf16[4,16,512]{2,1,0:T(8,128)(2,1)S(1)} %bitcast.55), channel_id=1, replica_groups=mesh['x'=4,'core'=2,'y'=4,'z'=8] {'y'}, dimensions={0} | all-to-all | bytes 131072 | tf_op jit(solution)/shard_map/all_to_all | solution.py:293
  19.1 0.7 pad_maximum_fusion.1
  19.8 19.1 %all_to_all.21 = f32[8,8,1152]{2,1,0:T(8,128)S(1)} all-to-all(f32[8,8,1152]{2,1,0:T(8,128)S(1)} %broadcast_in_dim.9), channel_id=1, replica_groups=mesh['x'=4,'core'=2,'y'=4,'z'=8] {'z'}, dimensions={0} | all-to-all | bytes 589824 | tf_op jit(solution)/shard_map/all_to_all | solution.py:279
  39.0 9.4 %all_to_all.22 = f32[4,8,2048]{2,1,0:T(8,128)S(1)} all-to-all(f32[4,8,2048]{2,1,0:T(8,128)S(1)} %broadcast_in_dim.10), channel_id=1, replica_groups=mesh['x'=4,'core'=2,'y'=4,'z'=8] {'y'}, dimensions={0} | all-to-all | bytes 524288 | tf_op jit(solution)/shard_map/all_to_all | solution.py:279
  48.4 1.1 broadcast_in_dim.11
  49.5 4.1 %all-to-all-start.3 = ((f32[4,4,8,2048]{3,2,1,0:T(8,128)}), f32[4,4,8,2048]{3,2,1,0:T(8,128)S(1)}, u32[]{:S(2)}, u32[]{:S(2)}) async-start(f32[4,4,8,2048]{3,2,1,0:T(8,128)} %broadcast_in_dim.11), calls=%async_computation.3 | async-start | bytes 2097152 | tf_op jit(solution)/shard_map/all_to_all | solution.py:279
  53.6 6.6 %collective-permute-start.1 = (bf16[4,16,512]{2,1,0:T(8,128)(2,1)S(1)}, bf16[4,16,512]{2,1,0:T(8,128)(2,1)S(1)}, u32[]{:S(2)}, u32[]{:S(2)}) collective-permute-start(bf16[4,16,512]{2,1,0:T(8,128)(2,1)S(1)} %all_to_all.20), channel_id=1, source_target_pairs={{0,0},{1,32},{2,64},{3,96},{4,128},{5,160},{6,192},{7,224},{8,8},{... | collective-permute-start | bytes 196616 | tf_op jit(solution)/shard_map/ppermute | solution.py:294
  60.2 3.5 %all-to-all-done.3.own_ref = f32[4,4,8,2048]{3,2,1,0:T(8,128)S(1)} async-done(((f32[4,4,8,2048]{3,2,1,0:T(8,128)}), f32[4,4,8,2048]{3,2,1,0:T(8,128)S(1)}, u32[]{:S(2)}, u32[]{:S(2)}) %all-to-all-start.3) | async-done | bytes 1048608 | tf_op jit(solution)/shard_map/all_to_all | solution.py:279
  63.7 0.0 copy-start
  63.7 5.9 %collective-permute-start = (f32[4,4,8,2048]{3,2,1,0:T(8,128)S(1)}, f32[4,4,8,2048]{3,2,1,0:T(8,128)}, u32[]{:S(2)}, u32[]{:S(2)}) collective-permute-start(f32[4,4,8,2048]{3,2,1,0:T(8,128)S(1)} %all-to-all-done.3.own_ref), channel_id=1, source_target_pairs={{0,32},{1,33},{2,34},{3,35},{4,36},{5,37},{6,38},{7,39},{8,40},{9,... | collective-permute-start | bytes 3145736 | tf_op jit(solution)/shard_map/ppermute | solution.py:303
  69.6 0.0 collective-permute-done.1
  69.7 0.0 copy-done.4
  69.7 0.1 collective-permute-start.2
  69.8 2.4 %collective-permute-done.2 = bf16[4,16,1536]{2,1,0:T(8,128)(2,1)S(1)} collective-permute-done((bf16[4,16,1536]{2,1,0:T(8,128)(2,1)S(1)}, bf16[4,16,1536]{2,1,0:T(8,128)(2,1)S(1)}, u32[]{:S(2)}, u32[]{:S(2)}) %collective-permute-start.2) | collective-permute-done | bytes 196640 | tf_op jit(solution)/shard_map/ppermute | solution.py:297
  72.2 0.0 copy-start.1
  72.3 2.4 %collective-permute-start.5 = (bf16[2,4,16,1536]{3,2,1,0:T(8,128)(2,1)S(1)}, bf16[2,4,16,1536]{3,2,1,0:T(8,128)(2,1)S(1)}, u32[]{:S(2)}, u32[]{:S(2)}) collective-permute-start(bf16[2,4,16,1536]{3,2,1,0:T(8,128)(2,1)S(1)} %pad_maximum_fusion.near0), channel_id=1, source_target_pairs={{0,192},{1,193},{2,194},{3,195},{4,196},{5,197},{6,198},{7,199},{8... | collective-permute-start | bytes 1179656 | tf_op jit(solution)/shard_map/ppermute | solution.py:304
  74.6 0.9 collective-permute-start.4
  75.6 0.8 collective-permute-start.3
  76.3 0.6 pad_add_fusion.place_ref
  77.0 0.0 collective-permute-done.other_ref
  77.0 0.0 copy-done
  77.0 28.0 %shard_map.42 = (f32[512,512]{1,0:T(8,128)}, bf16[512,512]{1,0:T(8,128)(2,1)}) custom-call(s32[1]{0:T(128)} %bitcast.3.core_ref, f32[4,4,8,2048]{3,2,1,0:T(8,128)} %copy-done, f32[4,4,8,2048]{3,2,1,0:T(8,128)} %collective-permute-done.other_ref), custom_call_target="tpu_custom_call" | custom-call | tf_op jit(solution)/shard_map/pallas_call | solution.py:192
  105.0 0.0 collective-permute-done.5.near3
  105.0 0.0 copy-start.2
  105.0 0.0 collective-permute-done.4.near2
  105.0 0.0 collective-permute-done.3.near1
  105.0 0.0 copy-done.1
  105.0 0.7 copy-done.2
  105.7 5.7 %shard_map.43 = (bf16[512,512]{1,0:T(8,128)(2,1)}, bf16[512,512]{1,0:T(8,128)(2,1)}, bf16[512,512]{1,0:T(8,128)(2,1)}, bf16[512,512]{1,0:T(8,128)(2,1)}, bf16[512,512]{1,0:T(8,128)(2,1)}) custom-call(s32[2]{0:T(128)} %pad_add_fusion.place_ref, f32[512,512]{1,0:T(8,128)} %get-tuple-element.16.inv_ref, bf16[512,512]{1,0:T(8,128)(2,1)} %get-tuple-element.17.first_ref.first, ...), custom_call_target="tpu_custom_call" | custom-call | tf_op jit(solution)/shard_map/pallas_call | solution.py:222
  111.4 0.0 all-gather.3.cloned.1.call-done
  111.4 14.1 %shard_map.44 = (f32[2048,512]{1,0:T(8,128)}, f32[16,2048]{1,0:T(8,128)}) custom-call(s32[1]{0:T(128)} %bitcast.col_ref, f32[2048,512]{1,0:T(8,128)} %normal_ref.1, bf16[32,12,16,512]{3,2,1,0:T(8,128)(2,1)} %bitcast.50, bf16[32,12,16,512]{3,2,1,0:T(8,128)(2,1)} %bitcast.51, bf16[32,12,16,512]{3,2,1,0:T(8,128)(2,1)} %bitcast.52, ...), custom_call_target="tpu_custom_call" | custom-call | tf_op jit(solution)/shard_map/pallas_call | solution.py:250
  (16 shorter events, 0.1 us)
Async XLA Ops:
  7.2 104.3 %all-gather.3.cloned.1.call-start = ((), (), s32[]{:S(2)}) async-start(), calls=%async_computation.4 | async-start | bytes 6488064 | tf_op jit(solution)/shard_map/all_gather | solution.py:292
  7.2 2.4 %copy-start.3 = (bf16[512,64]{0,1:T(8,128)(2,1)S(1)}, bf16[512,64]{0,1:T(8,128)(2,1)}, u32[]{:S(2)}) copy-start(bf16[512,64]{0,1:T(8,128)(2,1)} %param.3) | copy-start | bytes 196612
  9.6 60.1 %copy-start.4 = (bf16[4,16,1024]{2,1,0:T(8,128)(2,1)S(1)}, bf16[4,16,1024]{2,1,0:T(8,128)(2,1)}, u32[]{:S(2)}) copy-start(bf16[4,16,1024]{2,1,0:T(8,128)(2,1)} %get-tuple-element.18) | copy-start | bytes 393220
  49.5 14.3 %all-to-all-start.3 = ((f32[4,4,8,2048]{3,2,1,0:T(8,128)}), f32[4,4,8,2048]{3,2,1,0:T(8,128)S(1)}, u32[]{:S(2)}, u32[]{:S(2)}) async-start(f32[4,4,8,2048]{3,2,1,0:T(8,128)} %broadcast_in_dim.11), calls=%async_computation.3 | async-start | bytes 2097152 | tf_op jit(solution)/shard_map/all_to_all | solution.py:279
  53.6 16.1 %collective-permute-start.1 = (bf16[4,16,512]{2,1,0:T(8,128)(2,1)S(1)}, bf16[4,16,512]{2,1,0:T(8,128)(2,1)S(1)}, u32[]{:S(2)}, u32[]{:S(2)}) collective-permute-start(bf16[4,16,512]{2,1,0:T(8,128)(2,1)S(1)} %all_to_all.20), channel_id=1, source_target_pairs={{0,0},{1,32},{2,64},{3,96},{4,128},{5,160},{6,192},{7,224},{8,8},{... | collective-permute-start | bytes 196616 | tf_op jit(solution)/shard_map/ppermute | solution.py:294
  63.7 13.2 %copy-start = (f32[4,4,8,2048]{3,2,1,0:T(8,128)}, f32[4,4,8,2048]{3,2,1,0:T(8,128)S(1)}, u32[]{:S(2)}) copy-start(f32[4,4,8,2048]{3,2,1,0:T(8,128)S(1)} %all-to-all-done.3.own_ref) | copy-start | bytes 3145732
  63.7 13.2 %collective-permute-start = (f32[4,4,8,2048]{3,2,1,0:T(8,128)S(1)}, f32[4,4,8,2048]{3,2,1,0:T(8,128)}, u32[]{:S(2)}, u32[]{:S(2)}) collective-permute-start(f32[4,4,8,2048]{3,2,1,0:T(8,128)S(1)} %all-to-all-done.3.own_ref), channel_id=1, source_target_pairs={{0,32},{1,33},{2,34},{3,35},{4,36},{5,37},{6,38},{7,39},{8,40},{9,... | collective-permute-start | bytes 3145736 | tf_op jit(solution)/shard_map/ppermute | solution.py:303
  69.7 2.5 %collective-permute-start.2 = (bf16[4,16,1536]{2,1,0:T(8,128)(2,1)S(1)}, bf16[4,16,1536]{2,1,0:T(8,128)(2,1)S(1)}, u32[]{:S(2)}, u32[]{:S(2)}) collective-permute-start(bf16[4,16,1536]{2,1,0:T(8,128)(2,1)S(1)} %constant_dynamic-update-slice_fusion.8), channel_id=1, source_target_pairs={{0,32},{1,33},{2,34},{3,35},{4,36},{5,37},{6,38},{7,39},{8,40},{9,... | collective-permute-start | bytes 589832 | tf_op jit(solution)/shard_map/ppermute | solution.py:297
  72.2 32.8 %copy-start.1 = (bf16[2,4,16,1536]{3,2,1,0:T(8,128)(2,1)}, bf16[2,4,16,1536]{3,2,1,0:T(8,128)(2,1)S(1)}, u32[]{:S(2)}) copy-start(bf16[2,4,16,1536]{3,2,1,0:T(8,128)(2,1)S(1)} %pad_maximum_fusion.near0) | copy-start | bytes 1179652
  72.3 32.7 %collective-permute-start.5 = (bf16[2,4,16,1536]{3,2,1,0:T(8,128)(2,1)S(1)}, bf16[2,4,16,1536]{3,2,1,0:T(8,128)(2,1)S(1)}, u32[]{:S(2)}, u32[]{:S(2)}) collective-permute-start(bf16[2,4,16,1536]{3,2,1,0:T(8,128)(2,1)S(1)} %pad_maximum_fusion.near0), channel_id=1, source_target_pairs={{0,192},{1,193},{2,194},{3,195},{4,196},{5,197},{6,198},{7,199},{8... | collective-permute-start | bytes 1179656 | tf_op jit(solution)/shard_map/ppermute | solution.py:304
  74.6 30.4 %collective-permute-start.4 = (bf16[2,4,16,1536]{3,2,1,0:T(8,128)(2,1)S(1)}, bf16[2,4,16,1536]{3,2,1,0:T(8,128)(2,1)}, u32[]{:S(2)}, u32[]{:S(2)}) collective-permute-start(bf16[2,4,16,1536]{3,2,1,0:T(8,128)(2,1)S(1)} %pad_maximum_fusion.near0), channel_id=1, source_target_pairs={{0,128},{1,129},{2,130},{3,131},{4,132},{5,133},{6,134},{7,135},{8... | collective-permute-start | bytes 1179656 | tf_op jit(solution)/shard_map/ppermute | solution.py:304
  75.6 29.4 %collective-permute-start.3 = (bf16[2,4,16,1536]{3,2,1,0:T(8,128)(2,1)S(1)}, bf16[2,4,16,1536]{3,2,1,0:T(8,128)(2,1)}, u32[]{:S(2)}, u32[]{:S(2)}) collective-permute-start(bf16[2,4,16,1536]{3,2,1,0:T(8,128)(2,1)S(1)} %pad_maximum_fusion.near0), channel_id=1, source_target_pairs={{0,64},{1,65},{2,66},{3,67},{4,68},{5,69},{6,70},{7,71},{8,72},{9,... | collective-permute-start | bytes 1179656 | tf_op jit(solution)/shard_map/ppermute | solution.py:304
  105.0 0.7 copy-start.2
Sparse Core Ops, SparseCore 0:
  10.6 92.8 all-gather.2

commit v3 on v2

v3 whole, which is shorter than its diff:
```python
import functools

import jax
import jax.numpy as jnp
from jax import lax
from jax.experimental import pallas as pl
from jax.experimental.pallas import tpu as pltpu
from jax.sharding import Mesh
from jax.sharding import PartitionSpec as P

PW = 512
NB = 16
T = 128
AXES = ("x", "core", "y", "z")
F32 = jnp.float32
BF16 = jnp.bfloat16
HI = lax.Precision.HIGHEST
VMEM = pltpu.VMEM


def nt(a, b, precision=None):
    return lax.dot_general(a, b, (((1,), (1,)), ((), ())), precision=precision, preferred_element_type=F32)


def nn(a, b, precision=None):
    return lax.dot_general(a, b, (((1,), (0,)), ((), ())), precision=precision, preferred_element_type=F32)


def tn(a, b):
    return lax.dot_general(a, b, (((0,), (0,)), ((), ())), preferred_element_type=F32)


def split(x):
    high = x.astype(BF16)
    return high, (x - high.astype(F32)).astype(BF16)


def prep_kernel(cols_ref, rows_ref, jac_ref, wide_ref, corner_ref, near_ref):
    cols = cols_ref[...].T[:NB]
    high, low = split(cols)
    for q in range(4):
        wide_ref[q] = high[:, q * PW : (q + 1) * PW]
        wide_ref[4 + q] = low[:, q * PW : (q + 1) * PW]
        wide_ref[8 + q] = jac_ref[q * NB : (q + 1) * NB, :]
    corner = jnp.concatenate([cols[:8, :64], cols[8:, :64]], axis=1)
    first = corner.astype(BF16).astype(F32)
    second = (corner - first).astype(BF16).astype(F32)
    third = corner - first - second
    corner_ref[:, :T] = jnp.concatenate([first, second], axis=0).astype(BF16)
    corner_ref[:, T:] = jnp.concatenate([third, third], axis=0).astype(BF16)
    high, low = split(rows_ref[...])
    for i in range(4):
        near_ref[i, :, :PW] = high[i * NB : (i + 1) * NB]
        near_ref[i, :, PW:] = low[i * NB : (i + 1) * NB]


def prep(normal, jac_t):
    rows = normal.shape[0]
    return pl.pallas_call(
        prep_kernel,
        grid=(1,),
        in_specs=[
            pl.BlockSpec((rows, T), lambda i: (0, 0)),
            pl.BlockSpec((64, PW), lambda i: (0, 0)),
            pl.BlockSpec((64, PW), lambda i: (0, 0)),
        ],
        out_specs=[
            pl.BlockSpec((12, NB, PW), lambda i: (0, 0, 0)),
            pl.BlockSpec((NB, 2 * T), lambda i: (0, 0)),
            pl.BlockSpec((4, NB, 2 * PW), lambda i: (0, 0, 0)),
        ],
        out_shape=[
            jax.ShapeDtypeStruct((12, NB, PW), BF16),
            jax.ShapeDtypeStruct((NB, 2 * T), BF16),
            jax.ShapeDtypeStruct((4, NB, 2 * PW), BF16),
        ],
        compiler_params=pltpu.CompilerParams(vmem_limit_bytes=62 << 20),
    )(normal, normal, jac_t)


def factor_tile(tile):
    q = 8
    groups = T // q
    rows = [tile[q * i : q * (i + 1), :] for i in range(groups)]
    lane = lax.broadcasted_iota(jnp.int32, (q, T), 1)
    out = []
    spread = lambda v: jnp.broadcast_to(v, (q, T))
    for g in range(groups):
        base = g * q
        cols = {i: [spread(rows[i][:, base + l : base + l + 1]) for l in range(q)] for i in range(g, groups)}
        low = [[None] * q for _ in range(q)]
        r = [None] * q
        pivot = [[spread(cols[g][l][k : k + 1, :]) if k >= l else None for l in range(q)] for k in range(q)]
        inside = (lane >= base) & (lane < base + q)
        done = [
            jnp.where(inside, jnp.where(lane == base + l, 1.0, 0.0), spread(rows[g][l : l + 1, :])) for l in range(q)
        ]
        near = list(cols[g + 1]) if g + 1 < groups else None
        for j in range(q):
            r[j] = lax.rsqrt(pivot[j][j])
            done[j] = done[j] * r[j]
            for i in range(j + 1, q):
                low[i][j] = pivot[i][j] * r[j]
            for i in range(j + 1, q):
                for k in range(j + 1, i + 1):
                    pivot[i][k] = pivot[i][k] - low[i][j] * low[k][j]
                done[i] = done[i] - low[i][j] * done[j]
            if near:
                near[j] = near[j] * r[j]
                for k in range(j + 1, q):
                    near[k] = near[k] - low[k][j] * near[j]
        weight = list(done)
        for j in range(q - 1, -1, -1):
            weight[j] = weight[j] * r[j]
            for i in range(j):
                weight[i] = weight[i] - low[j][i] * weight[j]
        sub = lax.broadcasted_iota(jnp.int32, (q, T), 0)
        mine = done[0]
        for k in range(1, q):
            mine = jnp.where(sub >= k, done[k], mine)
        out.append(jnp.where(lane < base + q, mine, 0.0))
        for i in range(g + 1, groups):
            left, right = (near, done) if i == g + 1 else (cols[i], weight)
            acc = left[0] * right[0]
            for k in range(1, q):
                acc = acc + left[k] * right[k]
            rows[i] = jnp.where(inside, 0.0, rows[i]) - acc
    return jnp.concatenate(out, 0)


def factor(work, inv):
    inv[...] = jnp.zeros_like(inv)
    tiles = PW // T
    for b in range(tiles):
        lo, hi = b * T, (b + 1) * T
        here = factor_tile(work[lo:hi, lo:hi])
        inv[lo:hi, lo:hi] = here
        if b:
            inv[lo:hi, :lo] = nn(here, inv[lo:hi, :lo], HI)
        if b < tiles - 1:
            below = nt(work[hi:, lo:hi], here, HI)
            work[hi : hi + T, hi : hi + T] -= nt(below[:T], below[:T], HI)
            if b < tiles - 2:
                work[hi + T :, hi:] -= nt(below[T:], below, HI)
            inv[hi:, :hi] -= nn(below, inv[lo:hi, :hi], HI)


def place(refs, core, store):
    for x in range(4):
        for ref, r in ((refs[0], 2 * x + core), (refs[1], 2 * x + 1 - core)):
            for a in range(4):
                store(ref, x, a, r)


def tile_rows(a, r):
    return pl.ds(pl.multiple_of(a * T + r * NB, NB), NB)


def block_kernel(core_ref, own_ref, other_ref, inv_ref, first_ref, work, pieces):
    core = core_ref[0]

    def store(ref, x, a, r):
        upper, lower = ref[x, a, :, :PW], ref[x, a, :, PW : 2 * PW]
        first_ref[tile_rows(a, r), :] = jnp.concatenate([upper, lower], axis=0).astype(BF16)
        lanes = pl.ds(pl.multiple_of(r * T, T), T)
        for z in range(8):
            start = 2 * PW + z * T
            pieces[(a * 8 + z) * 8 : (a * 8 + z + 1) * 8, lanes] = ref[x, a, :, start : start + T]

    place((own_ref, other_ref), core, store)
    src = lax.broadcasted_iota(jnp.int32, (8 * T, PW), 0)
    dst = lax.broadcasted_iota(jnp.int32, (8 * T, PW), 1)
    to = (src // 16 % 4) * T + (src // T) * NB + src % NB
    high, rest = split(pieces[...])
    rest = pieces[...] - high.astype(F32)
    middle, low = split(rest)
    for half in range(2):
        move = jnp.where((to == dst) & (src // 64 % 2 == half), 1.0, 0.0).astype(BF16)
        part = nn(high, move) + nn(middle, move) + nn(low, move)
        work.reshape(32, 2, 8, PW)[:, half] = part.reshape(32, 8, PW)
    first = first_ref[...]
    work[...] += nt(first, first)
    factor(work, inv_ref)


def block(core, own, other):
    whole = pl.BlockSpec(memory_space=VMEM)
    return pl.pallas_call(
        block_kernel,
        in_specs=[pl.BlockSpec(memory_space=pltpu.SMEM), whole, whole],
        out_specs=[whole] * 2,
        out_shape=[jax.ShapeDtypeStruct((PW, PW), F32), jax.ShapeDtypeStruct((PW, PW), BF16)],
        scratch_shapes=[VMEM((PW, PW), F32), VMEM((256, 8 * T), F32)],
        compiler_params=pltpu.CompilerParams(vmem_limit_bytes=62 << 20),
    )(core, own, other)


def last_kernel(
    col_ref, normal, wide, first, inv, near, out, panel_out,
    normal_in, wide_in, first_in, inv_in, near_in, out_buf, gram, cols, save, sem, sem_const, sem_out,
):
    chunks = []
    for q in range(4):
        jac = pl.ds(8 * q, 8), pl.ds(8, 4)
        rows = pl.ds(q * PW, PW)
        chunks.append(
            [
                pltpu.make_async_copy(wide.at[jac], wide_in.at[jac], sem.at[q, 0]),
                pltpu.make_async_copy(wide.at[:, q], wide_in.at[:, q], sem.at[q, 1]),
                pltpu.make_async_copy(wide.at[:, 4 + q], wide_in.at[:, 4 + q], sem.at[q, 2]),
                pltpu.make_async_copy(normal.at[rows], normal_in.at[rows], sem.at[q, 3]),
            ]
        )
    const = [
        pltpu.make_async_copy(near, near_in, sem_const.at[0]),
        pltpu.make_async_copy(first, first_in, sem_const.at[1]),
        pltpu.make_async_copy(inv, inv_in, sem_const.at[2]),
    ]
    for copy in const + chunks[0]:
        copy.start()
    const[0].wait()
    for r in range(8):
        for a in range(4):
            at = slice(a * T + r * NB, a * T + (r + 1) * NB)
            cols[at, :] = near_in[r, a, :, :PW]
            gram[at, :] = near_in[r, a, :, PW : 2 * PW].astype(F32) + near_in[r, a, :, 2 * PW :].astype(F32)
    const[1].wait()
    right, rest = split(gram[...] + nt(first_in[...], cols[...]))
    const[2].wait()
    inv_hi, inv_lo = split(inv_in[...])
    far_hi, far_lo = split(nn(inv_hi, right) + (nn(inv_lo, right) + nn(inv_hi, rest)))
    moves_out = []
    at_panel = pl.ds(pl.multiple_of(col_ref[0] * NB, NB), NB)
    for q in range(4):
        for copy in chunks[q]:
            copy.wait()
        if q < 3:
            for copy in chunks[q + 1]:
                copy.start()
        rows = slice(q * PW, (q + 1) * PW)
        jac_rows = wide_in[8 * q : 8 * q + 8, 8:12].reshape(PW, PW)
        panel_in = wide_in[:, q].reshape(PW, PW).astype(F32) + wide_in[:, 4 + q].reshape(PW, PW).astype(F32)
        high, low = split(panel_in + nt(first_in[...], jac_rows))
        panel = nn(inv_hi, high) + (nn(inv_lo, high) + nn(inv_hi, low))
        save[...] = panel
        panel_out[:, rows] = save[at_panel, :]
        high, low = split(panel)
        drop = tn(high, far_hi) + (tn(low, far_hi) + tn(high, far_lo))
        out_buf[rows, :] = normal_in[rows, :] + nt(jac_rows, cols[...]) - drop
        moves_out.append(
            pltpu.make_async_copy(out_buf.at[pl.ds(q * PW, PW)], out.at[pl.ds(q * PW, PW)], sem_out.at[q])
        )
        moves_out[q].start()
    for copy in moves_out:
        copy.wait()


def last(col, normal, wide, first, inv, near):
    rows = normal.shape[0]
    there = pl.BlockSpec(memory_space=pl.ANY)
    return pl.pallas_call(
        last_kernel,
        in_specs=[pl.BlockSpec(memory_space=pltpu.SMEM)] + [there] * 5,
        out_specs=[there, pl.BlockSpec(memory_space=VMEM)],
        out_shape=[
            jax.ShapeDtypeStruct((rows, PW), F32),
            jax.ShapeDtypeStruct((NB, rows), F32),
        ],
        scratch_shapes=[
            VMEM((rows, PW), F32),
            VMEM((32, 12, NB, PW), BF16),
            VMEM((PW, PW), BF16),
            VMEM((PW, PW), F32),
            VMEM((8, 4, NB, 3 * PW), BF16),
            VMEM((rows, PW), F32),
            VMEM((PW, PW), F32),
            VMEM((PW, PW), BF16),
            VMEM((PW, PW), F32),
            pltpu.SemaphoreType.DMA((4, 4)),
            pltpu.SemaphoreType.DMA((3,)),
            pltpu.SemaphoreType.DMA((4,)),
        ],
        compiler_params=pltpu.CompilerParams(vmem_limit_bytes=62 << 20),
    )(col, normal, wide, first, inv, near)


def position(r, y, z):
    return (r * 4 + y) * 8 + z


def spread_over(value, axis, count):
    return lax.all_to_all(jnp.broadcast_to(value[None], (count,) + value.shape), axis, 0, 0, tiled=True)


def moves(to):
    return [(position(r, y, z), position(*to(r, y, z))) for r in range(8) for y in range(4) for z in range(8)]


def per_device(normal, jacobian):
    core = lax.axis_index("core").astype(jnp.int32)[None]
    col = (lax.axis_index("y") * 8 + lax.axis_index("z")).astype(jnp.int32)[None]
    jac_t = jacobian.T
    wide, corner, near = prep(normal, jac_t)
    wide = lax.all_gather(wide, ("y", "z"), axis=0, tiled=False)
    tiles = lax.all_to_all(jac_t.reshape(4, NB, PW), "y", 0, 0, tiled=True)
    swapped = lax.ppermute(tiles, AXES, moves(lambda r, y, z: (z, y, r)))
    near = jnp.concatenate([swapped, near], axis=2)
    got = spread_over(jnp.concatenate([tiles[0], corner], axis=1), "z", 8)
    head = got[0, :, :PW].astype(F32)
    parts = got[:, :, PW:].astype(F32)
    parts = parts[:, :8, :T] + parts[:, 8:, :T] + parts[:, :8, T:]
    sent = jnp.concatenate([head[:8], head[8:]] + [parts[z] for z in range(8)], axis=1)
    got = spread_over(sent, "y", 4)
    own = spread_over(got, "x", 4)
    other = lax.ppermute(own, AXES, moves(lambda r, y, z: (r ^ 1, y, z)))
    near = spread_over(near, ("x", "core"), 8)
    inv, first = block(core, own, other)
    updated, panel_t = last(col, normal, wide, first, inv, near)
    return updated, panel_t.T


def solution(mesh):
    fine = Mesh(mesh.devices.reshape(4, 2, 4, 8), AXES)
    rows, cols = ("x", "core"), ("y", "z")
    return jax.shard_map(
        per_device,
        mesh=fine,
        in_specs=(P(rows, cols), P(None, AXES)),
        out_specs=(P(rows, cols), P(rows, cols)),
        check_vma=False,
    )
```

time: 133 us -> 126 us (0.947)
  Pallas kernels: 50.2 us -> 42.3 us
  starting transfers between devices: 20.8 us -> 24.1 us
  blocking collectives: 37.9 us -> 34.9 us
    all_to_all x1 -> x2, starting transfers between devices: 4.12 us -> 16.6 us  [spread_over(): lax.all_to_all(jnp.broadcast_to(value[None], (count,) + value.shape), axi...]
    ppermute x5 -> x1, starting transfers between devices: 10.1 us -> 0.09 us  [per_device(): other = lax.ppermute(own, AXES, moves(lambda r, y, z: (r ^ 1, y, z)))]
    pallas_call x2 -> x1, Pallas kernels: 19.8 us -> 15.4 us  [last(): pl.pallas_call(last_kernel, in_specs=[pl.BlockSpec(memory_space=pltpu.SME...]
    pallas_call x1, Pallas kernels: 28 us -> 24.5 us  [block(): pl.pallas_call(block_kernel, in_specs=[pl.BlockSpec(memory_space=pltpu.SM...]
    all_to_all x1 -> x2, waiting for transfers between devices: 3.52 us -> 0.01 us  [spread_over(): lax.all_to_all(jnp.broadcast_to(value[None], (count,) + value.shape), axi...]
    all_to_all x2, blocking collectives: 28.5 us -> 25.5 us  [spread_over(): lax.all_to_all(jnp.broadcast_to(value[None], (count,) + value.shape), axi...]
    ppermute x1, waiting for transfers between devices: 0.01 us -> 2.64 us  [per_device(): swapped = lax.ppermute(tiles, AXES, moves(lambda r, y, z: (z, y, r)))]
    broadcast_in_dim x3 -> x4, local copies, waits for them, and re-layouts: 1.12 us -> 2.59 us  [spread_over(): jnp.broadcast_to(value[None], (count,) + value.shape)]
  transfers between devices with their start and end apart: 8 -> 5, of which waited for: 2 -> 3; matrix products, arithmetic and copies ran while one was open for 2% -> 3% of each run, Pallas kernels for 25% -> 20%
where the time goes in v3:
time: 126 us
  Pallas kernels  42.3 us (34%)
  blocking collectives  34.9 us (28%)
  starting transfers between devices  24.1 us (19%)
  between operations  14.2 us (11%)
  waiting for transfers between devices  6.21 us (5%)
  local copies, waits for them, and re-layouts  3.03 us (2%)
    all_to_all x2, blocking collectives, spread_over(): lax.all_to_all(jnp.broadcast_to(value[None], (count,) + value.shape), axi...  25.5 us
    pallas_call x1, Pallas kernels, block(): pl.pallas_call(block_kernel, in_specs=[pl.BlockSpec(memory_space=pltpu.SM...  24.5 us
    all_to_all x2, starting transfers between devices, spread_over(): lax.all_to_all(jnp.broadcast_to(value[None], (count,) + value.shape), axi...  16.6 us
    pallas_call x1, Pallas kernels, last(): pl.pallas_call(last_kernel, in_specs=[pl.BlockSpec(memory_space=pltpu.SME...  15.4 us
    all_to_all x1, blocking collectives, per_device(): tiles = lax.all_to_all(jac_t.reshape(4, NB, PW), 'y', 0, 0, tiled=True)  9.42 us
    ppermute x1, starting transfers between devices, per_device(): swapped = lax.ppermute(tiles, AXES, moves(lambda r, y, z: (z, y, r)))  7.38 us
    ppermute x1, waiting for transfers between devices, per_device(): other = lax.ppermute(own, AXES, moves(lambda r, y, z: (r ^ 1, y, z)))  2.7 us
    ppermute x1, waiting for transfers between devices, per_device(): swapped = lax.ppermute(tiles, AXES, moves(lambda r, y, z: (z, y, r)))  2.64 us
  transfers between devices with their start and end apart: 5, of which 3 were waited for; matrix products, arithmetic and copies ran while one was open for 3% of the time, Pallas kernels for 20%

profile of v3, /device:TPU:1, one launch (start us, length us, event | category | flops | bytes accessed | tf_op | source)
XLA Modules:
  0.0 125.5 jit_solution(8650294111371966702)
XLA Ops:
  7.2 0.0 all-gather.3.cloned.1.call-start
  7.2 0.0 copy-start.2
  7.2 2.4 %shard_map.41 = (bf16[12,16,512]{2,1,0:T(8,128)(2,1)}, bf16[16,256]{1,0:T(8,128)(2,1)}, bf16[4,16,1024]{2,1,0:T(8,128)(2,1)}) custom-call(f32[2048,512]{1,0:T(8,128)} %normal.1, f32[2048,512]{1,0:T(8,128)} %normal.1, bf16[64,512]{1,0:T(8,128)(2,1)} %bitcast.50), custom_call_target="tpu_custom_call" | custom-call | tf_op jit(solution)/shard_map/pallas_call | solution.py:59
  9.6 0.0 copy-start.3
  9.6 0.0 all-gather.3.cloned.1.call-update
  9.6 0.0 copy-done.2
  9.6 9.4 %all_to_all.25 = bf16[4,16,512]{2,1,0:T(8,128)(2,1)S(1)} all-to-all(bf16[4,16,512]{2,1,0:T(8,128)(2,1)S(1)} %bitcast.51), channel_id=1, replica_groups=mesh['x'=4,'core'=2,'y'=4,'z'=8] {'y'}, dimensions={0} | all-to-all | bytes 131072 | tf_op jit(solution)/shard_map/all_to_all | solution.py:305
  19.1 0.7 pad_maximum_fusion.1
  19.8 17.2 %all_to_all.26 = bf16[8,16,768]{2,1,0:T(8,128)(2,1)S(1)} all-to-all(bf16[8,16,768]{2,1,0:T(8,128)(2,1)S(1)} %broadcast_in_dim.14), channel_id=1, replica_groups=mesh['x'=4,'core'=2,'y'=4,'z'=8] {'z'}, dimensions={0} | all-to-all | bytes 393216 | tf_op jit(solution)/shard_map/all_to_all | solution.py:292
  37.1 8.4 %all_to_all.27 = f32[4,8,2048]{2,1,0:T(8,128)S(1)} all-to-all(f32[4,8,2048]{2,1,0:T(8,128)S(1)} %broadcast_in_dim.15), channel_id=1, replica_groups=mesh['x'=4,'core'=2,'y'=4,'z'=8] {'y'}, dimensions={0} | all-to-all | bytes 524288 | tf_op jit(solution)/shard_map/all_to_all | solution.py:292
  45.4 1.1 broadcast_in_dim.16
  46.5 4.0 %all-to-all-start.3 = ((f32[4,4,8,2048]{3,2,1,0:T(8,128)}), f32[4,4,8,2048]{3,2,1,0:T(8,128)S(1)}, u32[]{:S(2)}, u32[]{:S(2)}) async-start(f32[4,4,8,2048]{3,2,1,0:T(8,128)} %broadcast_in_dim.16), calls=%async_computation.3 | async-start | bytes 2097152 | tf_op jit(solution)/shard_map/all_to_all | solution.py:292
  50.5 7.4 %collective-permute-start.1 = (bf16[4,16,512]{2,1,0:T(8,128)(2,1)S(1)}, bf16[4,16,512]{2,1,0:T(8,128)(2,1)S(1)}, u32[]{:S(2)}, u32[]{:S(2)}) collective-permute-start(bf16[4,16,512]{2,1,0:T(8,128)(2,1)S(1)} %all_to_all.25), channel_id=1, source_target_pairs={{0,0},{1,32},{2,64},{3,96},{4,128},{5,160},{6,192},{7,224},{8,8},{... | collective-permute-start | bytes 196616 | tf_op jit(solution)/shard_map/ppermute | solution.py:306
  57.9 2.6 %collective-permute-done.1 = bf16[4,16,512]{2,1,0:T(8,128)(2,1)S(1)} collective-permute-done((bf16[4,16,512]{2,1,0:T(8,128)(2,1)S(1)}, bf16[4,16,512]{2,1,0:T(8,128)(2,1)S(1)}, u32[]{:S(2)}, u32[]{:S(2)}) %collective-permute-start.1) | collective-permute-done | bytes 65568 | tf_op jit(solution)/shard_map/ppermute | solution.py:306
  60.6 0.0 copy-done.3
  60.6 0.0 all-to-all-done.3.own_ref
  60.6 0.0 copy-start.1
  60.6 1.5 %broadcast_in_dim.17 = bf16[8,4,16,1536]{3,2,1,0:T(8,128)(2,1)} broadcast(bf16[4,16,1536]{2,1,0:T(8,128)(2,1)S(1)} %pad_maximum_fusion), dimensions={1,2,3} | broadcast | bytes 1769472 | tf_op jit(solution)/shard_map/broadcast_in_dim | solution.py:292
  62.1 12.6 %all-to-all-start.4 = ((bf16[8,4,16,1536]{3,2,1,0:T(8,128)(2,1)}), bf16[8,4,16,1536]{3,2,1,0:T(8,128)(2,1)S(1)}, u32[]{:S(2)}, u32[]{:S(2)}) async-start(bf16[8,4,16,1536]{3,2,1,0:T(8,128)(2,1)} %broadcast_in_dim.17), calls=%async_computation.4 | async-start | bytes 3145728 | tf_op jit(solution)/shard_map/all_to_all | solution.py:292
  74.7 0.0 copy-done.1
  74.7 0.1 collective-permute-start
  74.8 2.7 %collective-permute-done.other_ref = f32[4,4,8,2048]{3,2,1,0:T(8,128)} collective-permute-done((f32[4,4,8,2048]{3,2,1,0:T(8,128)S(1)}, f32[4,4,8,2048]{3,2,1,0:T(8,128)}, u32[]{:S(2)}, u32[]{:S(2)}) %collective-permute-start) | collective-permute-done | bytes 1048608 | tf_op jit(solution)/shard_map/ppermute | solution.py:315
  77.5 24.5 %shard_map.42 = (f32[512,512]{1,0:T(8,128)}, bf16[512,512]{1,0:T(8,128)(2,1)}) custom-call(s32[1]{0:T(128)} %bitcast.3.core_ref, f32[4,4,8,2048]{3,2,1,0:T(8,128)} %copy-done.1, f32[4,4,8,2048]{3,2,1,0:T(8,128)} %collective-permute-done.other_ref), custom_call_target="tpu_custom_call" | custom-call | tf_op jit(solution)/shard_map/pallas_call | solution.py:188
  102.0 0.0 all-to-all-done.4.near
  102.0 0.0 copy-start
  102.0 0.9 all-gather.3.cloned.1.call-done
  102.8 0.4 copy-done
  103.2 15.4 %shard_map.43 = (f32[2048,512]{1,0:T(8,128)}, f32[16,2048]{1,0:T(8,128)}) custom-call(s32[1]{0:T(128)} %bitcast.col_ref, f32[2048,512]{1,0:T(8,128)} %normal.1, bf16[32,12,16,512]{3,2,1,0:T(8,128)(2,1)} %bitcast.49, bf16[512,512]{1,0:T(8,128)(2,1)} %get-tuple-element.11.first, f32[512,512]{1,0:T(8,128)} %get-tuple-element.12.inv, ...), custom_call_target="tpu_custom_call" | custom-call | tf_op jit(solution)/shard_map/pallas_call | solution.py:261
  (17 shorter events, 0.1 us)
Async XLA Ops:
  7.2 95.7 %all-gather.3.cloned.1.call-start = ((), (), s32[]{:S(2)}) async-start(), calls=%async_computation.5 | async-start | bytes 6488064 | tf_op jit(solution)/shard_map/all_gather | solution.py:304
  7.2 2.4 %copy-start.2 = (bf16[512,64]{0,1:T(8,128)(2,1)S(1)}, bf16[512,64]{0,1:T(8,128)(2,1)}, u32[]{:S(2)}) copy-start(bf16[512,64]{0,1:T(8,128)(2,1)} %param.3) | copy-start | bytes 196612
  9.6 51.0 %copy-start.3 = (bf16[4,16,1024]{2,1,0:T(8,128)(2,1)S(1)}, bf16[4,16,1024]{2,1,0:T(8,128)(2,1)}, u32[]{:S(2)}) copy-start(bf16[4,16,1024]{2,1,0:T(8,128)(2,1)} %get-tuple-element.13) | copy-start | bytes 393220
  46.5 14.1 %all-to-all-start.3 = ((f32[4,4,8,2048]{3,2,1,0:T(8,128)}), f32[4,4,8,2048]{3,2,1,0:T(8,128)S(1)}, u32[]{:S(2)}, u32[]{:S(2)}) async-start(f32[4,4,8,2048]{3,2,1,0:T(8,128)} %broadcast_in_dim.16), calls=%async_computation.3 | async-start | bytes 2097152 | tf_op jit(solution)/shard_map/all_to_all | solution.py:292
  50.5 10.0 %collective-permute-start.1 = (bf16[4,16,512]{2,1,0:T(8,128)(2,1)S(1)}, bf16[4,16,512]{2,1,0:T(8,128)(2,1)S(1)}, u32[]{:S(2)}, u32[]{:S(2)}) collective-permute-start(bf16[4,16,512]{2,1,0:T(8,128)(2,1)S(1)} %all_to_all.25), channel_id=1, source_target_pairs={{0,0},{1,32},{2,64},{3,96},{4,128},{5,160},{6,192},{7,224},{8,8},{... | collective-permute-start | bytes 196616 | tf_op jit(solution)/shard_map/ppermute | solution.py:306
  60.6 14.1 %copy-start.1 = (f32[4,4,8,2048]{3,2,1,0:T(8,128)}, f32[4,4,8,2048]{3,2,1,0:T(8,128)S(1)}, u32[]{:S(2)}) copy-start(f32[4,4,8,2048]{3,2,1,0:T(8,128)S(1)} %all-to-all-done.3.own_ref) | copy-start | bytes 3145732
  62.1 39.9 %all-to-all-start.4 = ((bf16[8,4,16,1536]{3,2,1,0:T(8,128)(2,1)}), bf16[8,4,16,1536]{3,2,1,0:T(8,128)(2,1)S(1)}, u32[]{:S(2)}, u32[]{:S(2)}) async-start(bf16[8,4,16,1536]{3,2,1,0:T(8,128)(2,1)} %broadcast_in_dim.17), calls=%async_computation.4 | async-start | bytes 3145728 | tf_op jit(solution)/shard_map/all_to_all | solution.py:292
  74.7 2.8 %collective-permute-start = (f32[4,4,8,2048]{3,2,1,0:T(8,128)S(1)}, f32[4,4,8,2048]{3,2,1,0:T(8,128)}, u32[]{:S(2)}, u32[]{:S(2)}) collective-permute-start(f32[4,4,8,2048]{3,2,1,0:T(8,128)S(1)} %all-to-all-done.3.own_ref), channel_id=1, source_target_pairs={{0,32},{1,33},{2,34},{3,35},{4,36},{5,37},{6,38},{7,39},{8,40},{9,... | collective-permute-start | bytes 3145736 | tf_op jit(solution)/shard_map/ppermute | solution.py:315
  102.0 1.3 copy-start
Sparse Core Ops, SparseCore 0:
  10.6 92.2 all-gather.2

commit v4 on v3

--- a/solution.py
+++ b/solution.py
@@ -195,9 +195,53 @@
     )(core, own, other)
 
 
+def split3(x):
+    high, rest = x.astype(BF16), x - x.astype(BF16).astype(F32)
+    middle, low = split(rest)
+    return high, middle, low
+
+
+def far_kernel(col_ref, inv_ref, first_ref, near, w_hi, w_lo, v_hi, v_lo, own_rows, own_jac, cols, gram):
+    for r in range(8):
+        for a in range(4):
+            at = slice(a * T + r * NB, a * T + (r + 1) * NB)
+            cols[at, :] = near[r, a, :, :PW]
+            gram[at, :] = near[r, a, :, PW : 2 * PW].astype(F32) + near[r, a, :, 2 * PW :].astype(F32)
+    first = first_ref[...]
+    inv = inv_ref[...]
+    panel = nn(inv, gram[...] + nt(first, cols[...]), HI)
+    weight = nn(inv.T, panel, HI)
+    high, middle, low = split3(weight)
+    w_hi[...] = high
+    w_lo[...] = middle
+    change = tn(high, first) + (tn(middle, first) + tn(low, first))
+    high, low = split(cols[...].astype(F32) - change)
+    v_hi[...] = high
+    v_lo[...] = low
+    mine = inv_ref[pl.ds(pl.multiple_of(col_ref[0] * NB, NB), NB), :]
+    high, middle, low = split3(mine)
+    own_rows[:NB, :] = high
+    own_rows[NB:, :] = middle
+    high, low = split(nn(high, first) + (nn(middle, first) + nn(low, first)))
+    own_jac[:NB, :] = high
+    own_jac[NB:, :] = low
+
+
+def far(col, inv, first, near):
+    whole = pl.BlockSpec(memory_space=VMEM)
+    return pl.pallas_call(
+        far_kernel,
+        in_specs=[pl.BlockSpec(memory_space=pltpu.SMEM)] + [whole] * 3,
+        out_specs=[whole] * 6,
+        out_shape=[jax.ShapeDtypeStruct((PW, PW), BF16)] * 4 + [jax.ShapeDtypeStruct((2 * NB, PW), BF16)] * 2,
+        scratch_shapes=[VMEM((PW, PW), BF16), VMEM((PW, PW), F32)],
+        compiler_params=pltpu.CompilerParams(vmem_limit_bytes=62 << 20),
+    )(col, inv, first, near)
+
+
 def last_kernel(
-    col_ref, normal, wide, first, inv, near, out, panel_out,
-    normal_in, wide_in, first_in, inv_in, near_in, out_buf, gram, cols, save, sem, sem_const, sem_out,
+    normal, wide, w_hi, w_lo, v_hi, v_lo, own_rows, own_jac, out, panel_out,
+    normal_in, wide_in, w_hi_in, w_lo_in, v_hi_in, v_lo_in, out_buf, sem, sem_const, sem_out,
 ):
     chunks = []
     for q in range(4):
@@ -212,76 +256,65 @@
             ]
         )
     const = [
-        pltpu.make_async_copy(near, near_in, sem_const.at[0]),
-        pltpu.make_async_copy(first, first_in, sem_const.at[1]),
-        pltpu.make_async_copy(inv, inv_in, sem_const.at[2]),
+        pltpu.make_async_copy(src, dst, sem_const.at[k])
+        for k, (src, dst) in enumerate(((v_hi, v_hi_in), (v_lo, v_lo_in), (w_hi, w_hi_in), (w_lo, w_lo_in)))
     ]
-    for copy in const + chunks[0]:
+    for copy in (chunks[0][0], const[0], const[1], chunks[0][1], const[2], const[3], chunks[0][2], chunks[0][3]):
         copy.start()
-    const[0].wait()
-    for r in range(8):
-        for a in range(4):
-            at = slice(a * T + r * NB, a * T + (r + 1) * NB)
-            cols[at, :] = near_in[r, a, :, :PW]
-            gram[at, :] = near_in[r, a, :, PW : 2 * PW].astype(F32) + near_in[r, a, :, 2 * PW :].astype(F32)
-    const[1].wait()
-    right, rest = split(gram[...] + nt(first_in[...], cols[...]))
-    const[2].wait()
-    inv_hi, inv_lo = split(inv_in[...])
-    far_hi, far_lo = split(nn(inv_hi, right) + (nn(inv_lo, right) + nn(inv_hi, rest)))
     moves_out = []
-    at_panel = pl.ds(pl.multiple_of(col_ref[0] * NB, NB), NB)
     for q in range(4):
-        for copy in chunks[q]:
+        rows = slice(q * PW, (q + 1) * PW)
+        chunks[q][0].wait()
+        if q == 0:
+            const[0].wait()
+            const[1].wait()
+        jac_rows = wide_in[8 * q : 8 * q + 8, 8:12].reshape(PW, PW)
+        sums = nt(jac_rows, v_hi_in[...]) + nt(jac_rows, v_lo_in[...])
+        mine = nt(own_jac[...], jac_rows)
+        if q == 0:
+            const[2].wait()
+            const[3].wait()
+        for copy in chunks[q][1:]:
             copy.wait()
         if q < 3:
             for copy in chunks[q + 1]:
                 copy.start()
-        rows = slice(q * PW, (q + 1) * PW)
-        jac_rows = wide_in[8 * q : 8 * q + 8, 8:12].reshape(PW, PW)
-        panel_in = wide_in[:, q].reshape(PW, PW).astype(F32) + wide_in[:, 4 + q].reshape(PW, PW).astype(F32)
-        high, low = split(panel_in + nt(first_in[...], jac_rows))
-        panel = nn(inv_hi, high) + (nn(inv_lo, high) + nn(inv_hi, low))
-        save[...] = panel
-        panel_out[:, rows] = save[at_panel, :]
-        high, low = split(panel)
-        drop = tn(high, far_hi) + (tn(low, far_hi) + tn(high, far_lo))
-        out_buf[rows, :] = normal_in[rows, :] + nt(jac_rows, cols[...]) - drop
+        high = wide_in[:, q].reshape(PW, PW)
+        low = wide_in[:, 4 + q].reshape(PW, PW)
+        drop = tn(high, w_hi_in[...]) + (tn(low, w_hi_in[...]) + tn(high, w_lo_in[...]))
+        out_buf[rows, :] = normal_in[rows, :] + (sums - drop)
         moves_out.append(
             pltpu.make_async_copy(out_buf.at[pl.ds(q * PW, PW)], out.at[pl.ds(q * PW, PW)], sem_out.at[q])
         )
         moves_out[q].start()
+        mine = mine + nn(own_rows[...], high)
+        panel_out[:, rows] = mine[:NB] + mine[NB:] + nn(own_rows[:NB], low)
     for copy in moves_out:
         copy.wait()
 
 
-def last(col, normal, wide, first, inv, near):
+def last(normal, wide, w_hi, w_lo, v_hi, v_lo, own_rows, own_jac):
     rows = normal.shape[0]
     there = pl.BlockSpec(memory_space=pl.ANY)
+    whole = pl.BlockSpec(memory_space=VMEM)
     return pl.pallas_call(
         last_kernel,
-        in_specs=[pl.BlockSpec(memory_space=pltpu.SMEM)] + [there] * 5,
-        out_specs=[there, pl.BlockSpec(memory_space=VMEM)],
+        in_specs=[there] * 6 + [whole] * 2,
+        out_specs=[there, whole],
         out_shape=[
             jax.ShapeDtypeStruct((rows, PW), F32),
             jax.ShapeDtypeStruct((NB, rows), F32),
         ],
-        scratch_shapes=[
+        scratch_shapes=[VMEM((rows, PW), F32), VMEM((32, 12, NB, PW), BF16)]
+        + [VMEM((PW, PW), BF16)] * 4
+        + [
             VMEM((rows, PW), F32),
-            VMEM((32, 12, NB, PW), BF16),
-            VMEM((PW, PW), BF16),
-            VMEM((PW, PW), F32),
-            VMEM((8, 4, NB, 3 * PW), BF16),
-            VMEM((rows, PW), F32),
-            VMEM((PW, PW), F32),
-            VMEM((PW, PW), BF16),
-            VMEM((PW, PW), F32),
             pltpu.SemaphoreType.DMA((4, 4)),
-            pltpu.SemaphoreType.DMA((3,)),
             pltpu.SemaphoreType.DMA((4,)),
+            pltpu.SemaphoreType.DMA((4,)),
         ],
         compiler_params=pltpu.CompilerParams(vmem_limit_bytes=62 << 20),
-    )(col, normal, wide, first, inv, near)
+    )(normal, wide, w_hi, w_lo, v_hi, v_lo, own_rows, own_jac)
 
 
 def position(r, y, z):
@@ -310,12 +343,11 @@
     parts = got[:, :, PW:].astype(F32)
     parts = parts[:, :8, :T] + parts[:, 8:, :T] + parts[:, :8, T:]
     sent = jnp.concatenate([head[:8], head[8:]] + [parts[z] for z in range(8)], axis=1)
-    got = spread_over(sent, "y", 4)
-    own = spread_over(got, "x", 4)
+    own = spread_over(sent, ("x", "y"), 16).reshape(4, 4, 8, 4 * PW)
     other = lax.ppermute(own, AXES, moves(lambda r, y, z: (r ^ 1, y, z)))
     near = spread_over(near, ("x", "core"), 8)
     inv, first = block(core, own, other)
-    updated, panel_t = last(col, normal, wide, first, inv, near)
+    updated, panel_t = last(normal, wide, *far(col, inv, first, near))
     return updated, panel_t.T
 
 

time: 126 us -> 123 us (0.976)
  blocking collectives: 34.9 us -> 26.6 us
  Pallas kernels: 42.3 us -> 46.9 us
  waiting for transfers between devices: 6.21 us -> 9.53 us
  starting transfers between devices: 24.1 us -> 21.2 us
    all_to_all x2 -> x1, blocking collectives: 25.5 us -> 17.2 us  [spread_over(): lax.all_to_all(jnp.broadcast_to(value[None], (count,) + value.shape), axi...]
    pallas_call x1 -> x2, Pallas kernels: 15.4 us -> 20 us  [the longest x1 12.1 us: last(): pl.pallas_call(last_kernel, in_specs=[there] * 6 + [whole] * 2, out_specs...]
    all_to_all x2, waiting for transfers between devices: 0.01 us -> 2.1 us  [spread_over(): lax.all_to_all(jnp.broadcast_to(value[None], (count,) + value.shape), axi...]
    all_to_all x2, starting transfers between devices: 16.6 us -> 14.8 us  [spread_over(): lax.all_to_all(jnp.broadcast_to(value[None], (count,) + value.shape), axi...]
    broadcast_in_dim x4 -> x3, local copies, waits for them, and re-layouts: 2.59 us -> 2.53 us  [spread_over(): jnp.broadcast_to(value[None], (count,) + value.shape)]
  transfers between devices with their start and end apart: 5 -> 5, of which waited for: 3 -> 4; matrix products, arithmetic and copies ran while one was open for 3% -> 3% of each run, Pallas kernels for 20% -> 26%
where the time goes in v4:
time: 123 us
  Pallas kernels  46.9 us (38%)
  blocking collectives  26.6 us (22%)
  starting transfers between devices  21.2 us (17%)
  between operations  14.2 us (12%)
  waiting for transfers between devices  9.53 us (8%)
  local copies, waits for them, and re-layouts  3.72 us (3%)
    pallas_call x1, Pallas kernels, block(): pl.pallas_call(block_kernel, in_specs=[pl.BlockSpec(memory_space=pltpu.SM...  24.5 us
    all_to_all x1, blocking collectives, spread_over(): lax.all_to_all(jnp.broadcast_to(value[None], (count,) + value.shape), axi...  17.2 us
    all_to_all x2, starting transfers between devices, spread_over(): lax.all_to_all(jnp.broadcast_to(value[None], (count,) + value.shape), axi...  14.8 us
    pallas_call x1, Pallas kernels, last(): pl.pallas_call(last_kernel, in_specs=[there] * 6 + [whole] * 2, out_specs...  12.1 us
    all_to_all x1, blocking collectives, per_device(): tiles = lax.all_to_all(jac_t.reshape(4, NB, PW), 'y', 0, 0, tiled=True)  9.42 us
    pallas_call x1, Pallas kernels, far(): pl.pallas_call(far_kernel, in_specs=[pl.BlockSpec(memory_space=pltpu.SMEM...  7.99 us
    ppermute x1, starting transfers between devices, per_device(): swapped = lax.ppermute(tiles, AXES, moves(lambda r, y, z: (z, y, r)))  6.21 us
    ppermute x1, waiting for transfers between devices, per_device(): swapped = lax.ppermute(tiles, AXES, moves(lambda r, y, z: (z, y, r)))  3.62 us
  transfers between devices with their start and end apart: 5, of which 4 were waited for; matrix products, arithmetic and copies ran while one was open for 3% of the time, Pallas kernels for 26%

profile of v4, /device:TPU:1, one launch (start us, length us, event | category | flops | bytes accessed | tf_op | source)
XLA Modules:
  0.0 122.8 jit_solution(17487204863589203158)
XLA Ops:
  7.2 0.0 all-gather.3.cloned.1.call-start
  7.2 0.0 copy-start.2
  7.2 2.4 %shard_map.41 = (bf16[12,16,512]{2,1,0:T(8,128)(2,1)}, bf16[16,256]{1,0:T(8,128)(2,1)}, bf16[4,16,1024]{2,1,0:T(8,128)(2,1)}) custom-call(f32[2048,512]{1,0:T(8,128)} %normal.1, f32[2048,512]{1,0:T(8,128)} %normal.1, bf16[64,512]{1,0:T(8,128)(2,1)} %bitcast.53), custom_call_target="tpu_custom_call" | custom-call | tf_op jit(solution)/shard_map/pallas_call | solution.py:59
  9.6 0.0 copy-start.3
  9.6 0.0 all-gather.3.cloned.1.call-update
  9.6 0.0 copy-done.2
  9.6 9.4 %all_to_all.20 = bf16[4,16,512]{2,1,0:T(8,128)(2,1)S(1)} all-to-all(bf16[4,16,512]{2,1,0:T(8,128)(2,1)S(1)} %bitcast.54), channel_id=1, replica_groups=mesh['x'=4,'core'=2,'y'=4,'z'=8] {'y'}, dimensions={0} | all-to-all | bytes 131072 | tf_op jit(solution)/shard_map/all_to_all | solution.py:338
  19.1 0.7 pad_maximum_fusion.1
  19.8 17.2 %all_to_all.21 = bf16[8,16,768]{2,1,0:T(8,128)(2,1)S(1)} all-to-all(bf16[8,16,768]{2,1,0:T(8,128)(2,1)S(1)} %broadcast_in_dim.12), channel_id=1, replica_groups=mesh['x'=4,'core'=2,'y'=4,'z'=8] {'z'}, dimensions={0} | all-to-all | bytes 393216 | tf_op jit(solution)/shard_map/all_to_all | solution.py:325
  37.1 1.1 broadcast_in_dim.13
  38.1 4.7 %all-to-all-start.2 = ((f32[16,8,2048]{2,1,0:T(8,128)}), f32[16,8,2048]{2,1,0:T(8,128)S(1)}, u32[]{:S(2)}, u32[]{:S(2)}) async-start(f32[16,8,2048]{2,1,0:T(8,128)} %broadcast_in_dim.13), calls=%async_computation.2 | async-start | bytes 2097152 | tf_op jit(solution)/shard_map/all_to_all | solution.py:325
  42.9 6.2 %collective-permute-start.1 = (bf16[4,16,512]{2,1,0:T(8,128)(2,1)S(1)}, bf16[4,16,512]{2,1,0:T(8,128)(2,1)S(1)}, u32[]{:S(2)}, u32[]{:S(2)}) collective-permute-start(bf16[4,16,512]{2,1,0:T(8,128)(2,1)S(1)} %all_to_all.20), channel_id=1, source_target_pairs={{0,0},{1,32},{2,64},{3,96},{4,128},{5,160},{6,192},{7,224},{8,8},{... | collective-permute-start | bytes 196616 | tf_op jit(solution)/shard_map/ppermute | solution.py:339
  49.1 3.6 %collective-permute-done.1 = bf16[4,16,512]{2,1,0:T(8,128)(2,1)S(1)} collective-permute-done((bf16[4,16,512]{2,1,0:T(8,128)(2,1)S(1)}, bf16[4,16,512]{2,1,0:T(8,128)(2,1)S(1)}, u32[]{:S(2)}, u32[]{:S(2)}) %collective-permute-start.1) | collective-permute-done | bytes 65568 | tf_op jit(solution)/shard_map/ppermute | solution.py:339
  52.7 0.0 copy-done.3
  52.8 2.1 %all-to-all-done.2 = f32[16,8,2048]{2,1,0:T(8,128)S(1)} async-done(((f32[16,8,2048]{2,1,0:T(8,128)}), f32[16,8,2048]{2,1,0:T(8,128)S(1)}, u32[]{:S(2)}, u32[]{:S(2)}) %all-to-all-start.2) | async-done | bytes 1048608 | tf_op jit(solution)/shard_map/all_to_all | solution.py:325
  54.8 0.0 copy-start.1
  54.8 1.4 %broadcast_in_dim.28 = bf16[8,4,16,1536]{3,2,1,0:T(8,128)(2,1)} broadcast(bf16[4,16,1536]{2,1,0:T(8,128)(2,1)S(1)} %pad_maximum_fusion), dimensions={1,2,3} | broadcast | bytes 1769472 | tf_op jit(solution)/shard_map/broadcast_in_dim | solution.py:325
  56.3 10.1 %all-to-all-start.3 = ((bf16[8,4,16,1536]{3,2,1,0:T(8,128)(2,1)}), bf16[8,4,16,1536]{3,2,1,0:T(8,128)(2,1)S(1)}, u32[]{:S(2)}, u32[]{:S(2)}) async-start(bf16[8,4,16,1536]{3,2,1,0:T(8,128)(2,1)} %broadcast_in_dim.28), calls=%async_computation.3 | async-start | bytes 3145728 | tf_op jit(solution)/shard_map/all_to_all | solution.py:325
  66.4 0.0 copy-done.1
  66.4 0.1 collective-permute-start
  66.5 2.7 %collective-permute-done.other_ref = f32[4,4,8,2048]{3,2,1,0:T(8,128)} collective-permute-done((f32[4,4,8,2048]{3,2,1,0:T(8,128)S(1)}, f32[4,4,8,2048]{3,2,1,0:T(8,128)}, u32[]{:S(2)}, u32[]{:S(2)}) %collective-permute-start) | collective-permute-done | bytes 1048608 | tf_op jit(solution)/shard_map/ppermute | solution.py:347
  69.2 24.5 %shard_map.42 = (f32[512,512]{1,0:T(8,128)}, bf16[512,512]{1,0:T(8,128)(2,1)}) custom-call(s32[1]{0:T(128)} %bitcast.3.core_ref, f32[4,4,8,2048]{3,2,1,0:T(8,128)} %bitcast.52, f32[4,4,8,2048]{3,2,1,0:T(8,128)} %collective-permute-done.other_ref), custom_call_target="tpu_custom_call" | custom-call | tf_op jit(solution)/shard_map/pallas_call | solution.py:188
  93.7 0.0 all-to-all-done.3.near
  93.7 0.0 copy-start
  93.7 1.1 copy-done
  94.8 8.0 %shard_map.43 = (bf16[512,512]{1,0:T(8,128)(2,1)}, bf16[512,512]{1,0:T(8,128)(2,1)}, bf16[512,512]{1,0:T(8,128)(2,1)}, bf16[512,512]{1,0:T(8,128)(2,1)}, bf16[32...) custom-call(s32[1]{0:T(128)} %bitcast.2.col_ref, f32[512,512]{1,0:T(8,128)} %get-tuple-element.17.inv_ref, ...), custom_call_target="tpu_custom_call" | custom-call | tf_op jit(solution)/shard_map/pallas_call | solution.py:232
  102.8 1.1 all-gather.3.cloned.1.call-done
  103.9 12.1 %shard_map.44 = (f32[2048,512]{1,0:T(8,128)}, f32[16,2048]{1,0:T(8,128)}) custom-call(f32[2048,512]{1,0:T(8,128)} %normal.1, bf16[32,12,16,512]{3,2,1,0:T(8,128)(2,1)} %bitcast.50, bf16[512,512]{1,0:T(8,128)(2,1)} %get-tuple-element.20.w_hi, bf16[512,512]{1,0:T(8,128)(2,1)} %get-tuple-element.21.w_lo, bf16[512,512]{1,0:T(8,128)(2,1)} %get-tuple-element.22.v_hi, ...), custom_call_target="tpu_custom_call" | custom-call | tf_op jit(solution)/shard_map/pallas_call | solution.py:300
  (16 shorter events, 0.1 us)
Async XLA Ops:
  7.2 96.7 %all-gather.3.cloned.1.call-start = ((), (), s32[]{:S(2)}) async-start(), calls=%async_computation.4 | async-start | bytes 6488064 | tf_op jit(solution)/shard_map/all_gather | solution.py:337
  7.2 2.4 %copy-start.2 = (bf16[512,64]{0,1:T(8,128)(2,1)S(1)}, bf16[512,64]{0,1:T(8,128)(2,1)}, u32[]{:S(2)}) copy-start(bf16[512,64]{0,1:T(8,128)(2,1)} %param.3) | copy-start | bytes 196612
  9.6 43.1 %copy-start.3 = (bf16[4,16,1024]{2,1,0:T(8,128)(2,1)S(1)}, bf16[4,16,1024]{2,1,0:T(8,128)(2,1)}, u32[]{:S(2)}) copy-start(bf16[4,16,1024]{2,1,0:T(8,128)(2,1)} %get-tuple-element.19) | copy-start | bytes 393220
  38.1 16.7 %all-to-all-start.2 = ((f32[16,8,2048]{2,1,0:T(8,128)}), f32[16,8,2048]{2,1,0:T(8,128)S(1)}, u32[]{:S(2)}, u32[]{:S(2)}) async-start(f32[16,8,2048]{2,1,0:T(8,128)} %broadcast_in_dim.13), calls=%async_computation.2 | async-start | bytes 2097152 | tf_op jit(solution)/shard_map/all_to_all | solution.py:325
  42.9 9.8 %collective-permute-start.1 = (bf16[4,16,512]{2,1,0:T(8,128)(2,1)S(1)}, bf16[4,16,512]{2,1,0:T(8,128)(2,1)S(1)}, u32[]{:S(2)}, u32[]{:S(2)}) collective-permute-start(bf16[4,16,512]{2,1,0:T(8,128)(2,1)S(1)} %all_to_all.20), channel_id=1, source_target_pairs={{0,0},{1,32},{2,64},{3,96},{4,128},{5,160},{6,192},{7,224},{8,8},{... | collective-permute-start | bytes 196616 | tf_op jit(solution)/shard_map/ppermute | solution.py:339
  54.8 11.6 %copy-start.1 = (f32[16,8,2048]{2,1,0:T(8,128)}, f32[16,8,2048]{2,1,0:T(8,128)S(1)}, u32[]{:S(2)}) copy-start(f32[16,8,2048]{2,1,0:T(8,128)S(1)} %all-to-all-done.2) | copy-start | bytes 3145732
  56.3 37.4 %all-to-all-start.3 = ((bf16[8,4,16,1536]{3,2,1,0:T(8,128)(2,1)}), bf16[8,4,16,1536]{3,2,1,0:T(8,128)(2,1)S(1)}, u32[]{:S(2)}, u32[]{:S(2)}) async-start(bf16[8,4,16,1536]{3,2,1,0:T(8,128)(2,1)} %broadcast_in_dim.28), calls=%async_computation.3 | async-start | bytes 3145728 | tf_op jit(solution)/shard_map/all_to_all | solution.py:325
  66.4 2.8 %collective-permute-start = (f32[4,4,8,2048]{3,2,1,0:T(8,128)S(1)}, f32[4,4,8,2048]{3,2,1,0:T(8,128)}, u32[]{:S(2)}, u32[]{:S(2)}) collective-permute-start(f32[4,4,8,2048]{3,2,1,0:T(8,128)S(1)} %bitcast.51), channel_id=1, source_target_pairs={{0,32},{1,33},{2,34},{3,35},{4,36},{5,37},{6,38},{7,39},{8,40},{9,... | collective-permute-start | bytes 3145736 | tf_op jit(solution)/shard_map/ppermute | solution.py:347
  93.7 1.1 copy-start
Sparse Core Ops, SparseCore 0:
  10.6 93.2 all-gather.2

commit v5 on v4

--- a/solution.py
+++ b/solution.py
@@ -28,6 +28,14 @@
 
 def tn(a, b):
     return lax.dot_general(a, b, (((0,), (0,)), ((), ())), preferred_element_type=F32)
+
+
+def in_vmem(x):
+    return pltpu.with_memory_space_constraint(x, pltpu.VMEM)
+
+
+def in_hbm(x):
+    return pltpu.with_memory_space_constraint(x, pltpu.HBM)
 
 
 def split(x):
@@ -189,9 +197,9 @@
         block_kernel,
         in_specs=[pl.BlockSpec(memory_space=pltpu.SMEM), whole, whole],
         out_specs=[whole] * 2,
-        out_shape=[jax.ShapeDtypeStruct((PW, PW), F32), jax.ShapeDtypeStruct((PW, PW), BF16)],
+        out_shape=[VMEM((PW, PW), F32), jax.ShapeDtypeStruct((PW, PW), BF16)],
         scratch_shapes=[VMEM((PW, PW), F32), VMEM((256, 8 * T), F32)],
-        compiler_params=pltpu.CompilerParams(vmem_limit_bytes=62 << 20),
+        compiler_params=pltpu.CompilerParams(vmem_limit_bytes=48 << 20),
     )(core, own, other)
 
 
@@ -233,15 +241,17 @@
         far_kernel,
         in_specs=[pl.BlockSpec(memory_space=pltpu.SMEM)] + [whole] * 3,
         out_specs=[whole] * 6,
-        out_shape=[jax.ShapeDtypeStruct((PW, PW), BF16)] * 4 + [jax.ShapeDtypeStruct((2 * NB, PW), BF16)] * 2,
+        out_shape=[VMEM((PW, PW), BF16), jax.ShapeDtypeStruct((PW, PW), BF16)]
+        + [VMEM((PW, PW), BF16)] * 2
+        + [VMEM((2 * NB, PW), BF16)] * 2,
         scratch_shapes=[VMEM((PW, PW), BF16), VMEM((PW, PW), F32)],
-        compiler_params=pltpu.CompilerParams(vmem_limit_bytes=62 << 20),
-    )(col, inv, first, near)
+        compiler_params=pltpu.CompilerParams(vmem_limit_bytes=48 << 20),
+    )(col, in_vmem(inv), first, near)
 
 
 def last_kernel(
-    normal, wide, w_hi, w_lo, v_hi, v_lo, own_rows, own_jac, out, panel_out,
-    normal_in, wide_in, w_hi_in, w_lo_in, v_hi_in, v_lo_in, out_buf, sem, sem_const, sem_out,
+    normal, wide, w_lo, w_hi, v_hi, v_lo, own_rows, own_jac, out, panel_out,
+    wide_in, normal_in, w_lo_in, out_buf, sem, sem_w, sem_out,
 ):
     chunks = []
     for q in range(4):
@@ -255,33 +265,24 @@
                 pltpu.make_async_copy(normal.at[rows], normal_in.at[rows], sem.at[q, 3]),
             ]
         )
-    const = [
-        pltpu.make_async_copy(src, dst, sem_const.at[k])
-        for k, (src, dst) in enumerate(((v_hi, v_hi_in), (v_lo, v_lo_in), (w_hi, w_hi_in), (w_lo, w_lo_in)))
-    ]
-    for copy in (chunks[0][0], const[0], const[1], chunks[0][1], const[2], const[3], chunks[0][2], chunks[0][3]):
+    copy_w = pltpu.make_async_copy(w_lo, w_lo_in, sem_w)
+    for copy in chunks[0][:3] + [copy_w] + chunks[0][3:]:
         copy.start()
     moves_out = []
     for q in range(4):
         rows = slice(q * PW, (q + 1) * PW)
         chunks[q][0].wait()
-        if q == 0:
-            const[0].wait()
-            const[1].wait()
         jac_rows = wide_in[8 * q : 8 * q + 8, 8:12].reshape(PW, PW)
-        sums = nt(jac_rows, v_hi_in[...]) + nt(jac_rows, v_lo_in[...])
+        sums = nt(jac_rows, v_hi[...]) + nt(jac_rows, v_lo[...])
         mine = nt(own_jac[...], jac_rows)
-        if q == 0:
-            const[2].wait()
-            const[3].wait()
-        for copy in chunks[q][1:]:
+        for copy in chunks[q][1:] + [copy_w] * (q == 0):
             copy.wait()
         if q < 3:
             for copy in chunks[q + 1]:
                 copy.start()
         high = wide_in[:, q].reshape(PW, PW)
         low = wide_in[:, 4 + q].reshape(PW, PW)
-        drop = tn(high, w_hi_in[...]) + (tn(low, w_hi_in[...]) + tn(high, w_lo_in[...]))
+        drop = tn(high, w_hi[...]) + (tn(low, w_hi[...]) + tn(high, w_lo_in[...]))
         out_buf[rows, :] = normal_in[rows, :] + (sums - drop)
         moves_out.append(
             pltpu.make_async_copy(out_buf.at[pl.ds(q * PW, PW)], out.at[pl.ds(q * PW, PW)], sem_out.at[q])
@@ -293,28 +294,29 @@
         copy.wait()
 
 
-def last(normal, wide, w_hi, w_lo, v_hi, v_lo, own_rows, own_jac):
+def last(normal, wide, w_hi, w_lo, *parts):
     rows = normal.shape[0]
     there = pl.BlockSpec(memory_space=pl.ANY)
     whole = pl.BlockSpec(memory_space=VMEM)
     return pl.pallas_call(
         last_kernel,
-        in_specs=[there] * 6 + [whole] * 2,
+        in_specs=[there] * 3 + [whole] * 5,
         out_specs=[there, whole],
         out_shape=[
             jax.ShapeDtypeStruct((rows, PW), F32),
             jax.ShapeDtypeStruct((NB, rows), F32),
         ],
-        scratch_shapes=[VMEM((rows, PW), F32), VMEM((32, 12, NB, PW), BF16)]
-        + [VMEM((PW, PW), BF16)] * 4
-        + [
+        scratch_shapes=[
+            VMEM((32, 12, NB, PW), BF16),
+            VMEM((rows, PW), F32),
+            VMEM((PW, PW), BF16),
             VMEM((rows, PW), F32),
             pltpu.SemaphoreType.DMA((4, 4)),
+            pltpu.SemaphoreType.DMA,
             pltpu.SemaphoreType.DMA((4,)),
-            pltpu.SemaphoreType.DMA((4,)),
-        ],
-        compiler_params=pltpu.CompilerParams(vmem_limit_bytes=62 << 20),
-    )(normal, wide, w_hi, w_lo, v_hi, v_lo, own_rows, own_jac)
+        ],
+        compiler_params=pltpu.CompilerParams(vmem_limit_bytes=48 << 20),
+    )(in_hbm(normal), in_hbm(wide), in_hbm(w_lo), in_vmem(w_hi), *(in_vmem(part) for part in parts))
 
 
 def position(r, y, z):

time: 123 us -> 122 us (level)
  Pallas kernels: 46.9 us -> 41.4 us
  local copies, waits for them, and re-layouts: 3.72 us -> 7.3 us
    unnamed x17 -> x23, local copies, waits for them, and re-layouts: 1.18 us -> 4.89 us
    pallas_call x1, Pallas kernels: 7.99 us -> 5.14 us  [far(): pl.pallas_call(far_kernel, in_specs=[pl.BlockSpec(memory_space=pltpu.SMEM...]
    pallas_call x1, Pallas kernels: 24.5 us -> 23.1 us  [block(): pl.pallas_call(block_kernel, in_specs=[pl.BlockSpec(memory_space=pltpu.SM...]
    pallas_call x1, Pallas kernels: 12.1 us -> 10.8 us  [last(): pl.pallas_call(last_kernel, in_specs=[there] * 3 + [whole] * 5, out_specs...]
  transfers between devices with their start and end apart: 5 -> 5, of which waited for: 4 -> 4; matrix products, arithmetic and copies ran while one was open for 3% -> 3% of each run, Pallas kernels for 26% -> 23%
where the time goes in v5:
time: 122 us
  Pallas kernels  41.4 us (34%)
  blocking collectives  26.6 us (22%)
  starting transfers between devices  21 us (17%)
  between operations  14.2 us (12%)
  waiting for transfers between devices  10.4 us (9%)
  local copies, waits for them, and re-layouts  7.3 us (6%)
    pallas_call x1, Pallas kernels, block(): pl.pallas_call(block_kernel, in_specs=[pl.BlockSpec(memory_space=pltpu.SM...  23.1 us
    all_to_all x1, blocking collectives, spread_over(): lax.all_to_all(jnp.broadcast_to(value[None], (count,) + value.shape), axi...  17.2 us
    all_to_all x2, starting transfers between devices, spread_over(): lax.all_to_all(jnp.broadcast_to(value[None], (count,) + value.shape), axi...  14.7 us
    pallas_call x1, Pallas kernels, last(): pl.pallas_call(last_kernel, in_specs=[there] * 3 + [whole] * 5, out_specs...  10.8 us
    all_to_all x1, blocking collectives, per_device(): tiles = lax.all_to_all(jac_t.reshape(4, NB, PW), 'y', 0, 0, tiled=True)  9.42 us
    ppermute x1, starting transfers between devices, per_device(): swapped = lax.ppermute(tiles, AXES, moves(lambda r, y, z: (z, y, r)))  6.19 us
    pallas_call x1, Pallas kernels, far(): pl.pallas_call(far_kernel, in_specs=[pl.BlockSpec(memory_space=pltpu.SMEM...  5.14 us
    unnamed x23, local copies, waits for them, and re-layouts  4.89 us
  transfers between devices with their start and end apart: 5, of which 4 were waited for; matrix products, arithmetic and copies ran while one was open for 3% of the time, Pallas kernels for 23%

profile of v5, /device:TPU:1, one launch (start us, length us, event | category | flops | bytes accessed | tf_op | source)
XLA Modules:
  0.0 121.6 jit_solution(2408531290187335534)
XLA Ops:
  7.2 0.0 all-gather.3.cloned.1.call-start
  7.2 0.0 copy-start.5
  7.2 2.4 %shard_map.41 = (bf16[12,16,512]{2,1,0:T(8,128)(2,1)}, bf16[16,256]{1,0:T(8,128)(2,1)}, bf16[4,16,1024]{2,1,0:T(8,128)(2,1)}) custom-call(f32[2048,512]{1,0:T(8,128)} %normal.1, f32[2048,512]{1,0:T(8,128)} %normal.1, bf16[64,512]{1,0:T(8,128)(2,1)} %bitcast.53), custom_call_target="tpu_custom_call" | custom-call | tf_op jit(solution)/shard_map/pallas_call | solution.py:67
  9.6 0.0 copy-start.6
  9.6 0.0 all-gather.3.cloned.1.call-update
  9.6 0.0 copy-done.5
  9.7 9.4 %all_to_all.20 = bf16[4,16,512]{2,1,0:T(8,128)(2,1)S(1)} all-to-all(bf16[4,16,512]{2,1,0:T(8,128)(2,1)S(1)} %bitcast.54), channel_id=1, replica_groups=mesh['x'=4,'core'=2,'y'=4,'z'=8] {'y'}, dimensions={0} | all-to-all | bytes 131072 | tf_op jit(solution)/shard_map/all_to_all | solution.py:340
  19.1 0.7 pad_maximum_fusion.1
  19.8 17.2 %all_to_all.21 = bf16[8,16,768]{2,1,0:T(8,128)(2,1)S(1)} all-to-all(bf16[8,16,768]{2,1,0:T(8,128)(2,1)S(1)} %broadcast_in_dim.12), channel_id=1, replica_groups=mesh['x'=4,'core'=2,'y'=4,'z'=8] {'z'}, dimensions={0} | all-to-all | bytes 393216 | tf_op jit(solution)/shard_map/all_to_all | solution.py:327
  37.1 1.1 broadcast_in_dim.13
  38.2 4.8 %all-to-all-start.2 = ((f32[16,8,2048]{2,1,0:T(8,128)}), f32[16,8,2048]{2,1,0:T(8,128)S(1)}, u32[]{:S(2)}, u32[]{:S(2)}) async-start(f32[16,8,2048]{2,1,0:T(8,128)} %broadcast_in_dim.13), calls=%async_computation.2 | async-start | bytes 2097152 | tf_op jit(solution)/shard_map/all_to_all | solution.py:327
  42.9 6.2 %collective-permute-start.1 = (bf16[4,16,512]{2,1,0:T(8,128)(2,1)S(1)}, bf16[4,16,512]{2,1,0:T(8,128)(2,1)S(1)}, u32[]{:S(2)}, u32[]{:S(2)}) collective-permute-start(bf16[4,16,512]{2,1,0:T(8,128)(2,1)S(1)} %all_to_all.20), channel_id=1, source_target_pairs={{0,0},{1,32},{2,64},{3,96},{4,128},{5,160},{6,192},{7,224},{8,8},{... | collective-permute-start | bytes 196616 | tf_op jit(solution)/shard_map/ppermute | solution.py:341
  49.1 3.6 %collective-permute-done.1 = bf16[4,16,512]{2,1,0:T(8,128)(2,1)S(1)} collective-permute-done((bf16[4,16,512]{2,1,0:T(8,128)(2,1)S(1)}, bf16[4,16,512]{2,1,0:T(8,128)(2,1)S(1)}, u32[]{:S(2)}, u32[]{:S(2)}) %collective-permute-start.1) | collective-permute-done | bytes 65568 | tf_op jit(solution)/shard_map/ppermute | solution.py:341
  52.7 0.0 copy-done.6
  52.7 2.2 %all-to-all-done.2 = f32[16,8,2048]{2,1,0:T(8,128)S(1)} async-done(((f32[16,8,2048]{2,1,0:T(8,128)}), f32[16,8,2048]{2,1,0:T(8,128)S(1)}, u32[]{:S(2)}, u32[]{:S(2)}) %all-to-all-start.2) | async-done | bytes 1048608 | tf_op jit(solution)/shard_map/all_to_all | solution.py:327
  54.9 1.3 %broadcast_in_dim.28 = bf16[8,4,16,1536]{3,2,1,0:T(8,128)(2,1)} broadcast(bf16[4,16,1536]{2,1,0:T(8,128)(2,1)S(1)} %pad_maximum_fusion), dimensions={1,2,3} | broadcast | bytes 1769472 | tf_op jit(solution)/shard_map/broadcast_in_dim | solution.py:327
  56.2 9.9 %all-to-all-start.3 = ((bf16[8,4,16,1536]{3,2,1,0:T(8,128)(2,1)}), bf16[8,4,16,1536]{3,2,1,0:T(8,128)(2,1)S(1)}, u32[]{:S(2)}, u32[]{:S(2)}) async-start(bf16[8,4,16,1536]{3,2,1,0:T(8,128)(2,1)} %broadcast_in_dim.28), calls=%async_computation.3 | async-start | bytes 3145728 | tf_op jit(solution)/shard_map/all_to_all | solution.py:327
  66.2 0.0 collective-permute-start
  66.2 2.8 %collective-permute-done.other_ref = f32[4,4,8,2048]{3,2,1,0:T(8,128)} collective-permute-done((f32[4,4,8,2048]{3,2,1,0:T(8,128)S(1)}, f32[4,4,8,2048]{3,2,1,0:T(8,128)}, u32[]{:S(2)}, u32[]{:S(2)}) %collective-permute-start) | collective-permute-done | bytes 1048608 | tf_op jit(solution)/shard_map/ppermute | solution.py:349
  69.0 23.1 %shard_map.42 = (f32[512,512]{1,0:T(8,128)S(1)}, bf16[512,512]{1,0:T(8,128)(2,1)S(1)}) custom-call(s32[1]{0:T(128)} %bitcast.3.core_ref, f32[4,4,8,2048]{3,2,1,0:T(8,128)S(1)} %bitcast.51, f32[4,4,8,2048]{3,2,1,0:T(8,128)} %collective-permute-done.other_ref), custom_call_target="tpu_custom_call" | custom-call | tf_op jit(solution)/shard_map/pallas_call | solution.py:196
  92.0 0.0 copy-start
  92.1 1.0 copy-done
  93.0 0.0 copy-start.3
  93.0 0.8 copy-done.3
  93.8 0.0 all-to-all-done.3.near
  93.8 0.0 copy-start.1
  93.8 1.2 %copy-done.1 = f32[512,512]{1,0:T(8,128)S(1)} copy-done((f32[512,512]{1,0:T(8,128)S(1)}, f32[512,512]{1,0:T(8,128)}, u32[]{:S(2)}) %copy-start.1) | copy-done | bytes 1048600
  95.1 0.0 copy-start.4
  95.1 1.0 copy-done.4
  96.1 5.1 %shard_map.43 = (bf16[512,512]{1,0:T(8,128)(2,1)S(1)}, bf16[512,512]{1,0:T(8,128)(2,1)S(1)}, bf16[512,512]{1,0:T(8,128)(2,1)S(1)}, bf16[512,512]{1,0:T(8,128)(2,...) custom-call(s32[1]{0:T(128)} %bitcast.2.col_ref, f32[512,512]{1,0:T(8,128)S(1)} %copy-done.1, ...), custom_call_target="tpu_custom_call" | custom-call | tf_op jit(solution)/shard_map/pallas_call | solution.py:240
  101.3 0.0 copy-start.2
  101.3 0.8 copy-done.2
  102.1 1.9 %all-gather.3.cloned.1.call-done = bf16[384,16,512]{2,1,0:T(8,128)(2,1)} async-done(((bf16[12,16,512]{2,1,0:T(8,128)(2,1)}), bf16[384,16,512]{2,1,0:T(8,128)(2,1)}) %all-gather.3.cloned.1.call-update) | async-done | bytes 6291472 | tf_op jit(solution)/shard_map/all_gather | solution.py:339
  103.9 10.8 %shard_map.44 = (f32[2048,512]{1,0:T(8,128)}, f32[16,2048]{1,0:T(8,128)}) custom-call(f32[2048,512]{1,0:T(8,128)} %normal.1, bf16[32,12,16,512]{3,2,1,0:T(8,128)(2,1)} %bitcast.52, bf16[512,512]{1,0:T(8,128)(2,1)} %copy-done.2, bf16[512,512]{1,0:T(8,128)(2,1)S(1)} %get-tuple-element.21.w_hi, bf16[512,512]{1,0:T(8,128)(2,1)S(1)} %get-tuple-element.22.v_hi, ...), custom_call_target="tpu_custom_call" | custom-call | tf_op jit(solution)/shard_map/pallas_call | solution.py:301
  (16 shorter events, 0.1 us)
Async XLA Ops:
  7.2 96.8 %all-gather.3.cloned.1.call-start = ((), (), s32[]{:S(2)}) async-start(), calls=%async_computation.4 | async-start | bytes 6488064 | tf_op jit(solution)/shard_map/all_gather | solution.py:339
  7.2 2.4 %copy-start.5 = (bf16[512,64]{0,1:T(8,128)(2,1)S(1)}, bf16[512,64]{0,1:T(8,128)(2,1)}, u32[]{:S(2)}) copy-start(bf16[512,64]{0,1:T(8,128)(2,1)} %param.3) | copy-start | bytes 196612
  9.6 43.1 %copy-start.6 = (bf16[4,16,1024]{2,1,0:T(8,128)(2,1)S(1)}, bf16[4,16,1024]{2,1,0:T(8,128)(2,1)}, u32[]{:S(2)}) copy-start(bf16[4,16,1024]{2,1,0:T(8,128)(2,1)} %get-tuple-element.19) | copy-start | bytes 393220
  38.2 16.7 %all-to-all-start.2 = ((f32[16,8,2048]{2,1,0:T(8,128)}), f32[16,8,2048]{2,1,0:T(8,128)S(1)}, u32[]{:S(2)}, u32[]{:S(2)}) async-start(f32[16,8,2048]{2,1,0:T(8,128)} %broadcast_in_dim.13), calls=%async_computation.2 | async-start | bytes 2097152 | tf_op jit(solution)/shard_map/all_to_all | solution.py:327
  42.9 9.8 %collective-permute-start.1 = (bf16[4,16,512]{2,1,0:T(8,128)(2,1)S(1)}, bf16[4,16,512]{2,1,0:T(8,128)(2,1)S(1)}, u32[]{:S(2)}, u32[]{:S(2)}) collective-permute-start(bf16[4,16,512]{2,1,0:T(8,128)(2,1)S(1)} %all_to_all.20), channel_id=1, source_target_pairs={{0,0},{1,32},{2,64},{3,96},{4,128},{5,160},{6,192},{7,224},{8,8},{... | collective-permute-start | bytes 196616 | tf_op jit(solution)/shard_map/ppermute | solution.py:341
  56.2 37.6 %all-to-all-start.3 = ((bf16[8,4,16,1536]{3,2,1,0:T(8,128)(2,1)}), bf16[8,4,16,1536]{3,2,1,0:T(8,128)(2,1)S(1)}, u32[]{:S(2)}, u32[]{:S(2)}) async-start(bf16[8,4,16,1536]{3,2,1,0:T(8,128)(2,1)} %broadcast_in_dim.28), calls=%async_computation.3 | async-start | bytes 3145728 | tf_op jit(solution)/shard_map/all_to_all | solution.py:327
  66.2 2.8 %collective-permute-start = (f32[4,4,8,2048]{3,2,1,0:T(8,128)S(1)}, f32[4,4,8,2048]{3,2,1,0:T(8,128)}, u32[]{:S(2)}, u32[]{:S(2)}) collective-permute-start(f32[4,4,8,2048]{3,2,1,0:T(8,128)S(1)} %bitcast.50), channel_id=1, source_target_pairs={{0,32},{1,33},{2,34},{3,35},{4,36},{5,37},{6,38},{7,39},{8,40},{9,... | collective-permute-start | bytes 3145736 | tf_op jit(solution)/shard_map/ppermute | solution.py:349
  92.0 1.0 copy-start
  93.0 0.8 copy-start.3
  93.8 1.2 %copy-start.1 = (f32[512,512]{1,0:T(8,128)S(1)}, f32[512,512]{1,0:T(8,128)}, u32[]{:S(2)}) copy-start(f32[512,512]{1,0:T(8,128)} %copy-done) | copy-start | bytes 3145732
  95.1 1.1 copy-start.4
  101.3 0.8 copy-start.2
Sparse Core Ops, SparseCore 0:
  10.6 93.3 all-gather.2

commit v6 on v5

--- a/solution.py
+++ b/solution.py
@@ -43,14 +43,33 @@
     return high, (x - high.astype(F32)).astype(BF16)
 
 
-def prep_kernel(cols_ref, rows_ref, jac_ref, wide_ref, corner_ref, near_ref):
-    cols = cols_ref[...].T[:NB]
-    high, low = split(cols)
-    for q in range(4):
-        wide_ref[q] = high[:, q * PW : (q + 1) * PW]
-        wide_ref[4 + q] = low[:, q * PW : (q + 1) * PW]
-        wide_ref[8 + q] = jac_ref[q * NB : (q + 1) * NB, :]
-    corner = jnp.concatenate([cols[:8, :64], cols[8:, :64]], axis=1)
+def wide_kernel(cols_ref, jac_ref, wide_ref):
+    high, low = split(cols_ref[...].T[:NB])
+    for q in range(2):
+        wide_ref[0, q] = high[:, q * PW : (q + 1) * PW]
+        wide_ref[1, q] = low[:, q * PW : (q + 1) * PW]
+        wide_ref[2, q] = jac_ref[q * NB : (q + 1) * NB, :]
+
+
+def prep_wide(normal, jac_t):
+    rows = normal.shape[0]
+    parts = pl.pallas_call(
+        wide_kernel,
+        grid=(2,),
+        in_specs=[
+            pl.BlockSpec((rows // 2, T), lambda i: (i, 0)),
+            pl.BlockSpec((2 * NB, PW), lambda i: (i, 0)),
+        ],
+        out_specs=pl.BlockSpec((3, 2, NB, PW), lambda i: (0, i, 0, 0)),
+        out_shape=jax.ShapeDtypeStruct((3, 4, NB, PW), BF16),
+        compiler_params=pltpu.CompilerParams(vmem_limit_bytes=62 << 20),
+    )(normal, jac_t)
+    return parts.reshape(12, NB, PW)
+
+
+def near_kernel(rows_ref, corner_ref, near_ref):
+    cols = rows_ref[:, :T].T[:NB]
+    corner = jnp.concatenate([cols[:8], cols[8:]], axis=1)
     first = corner.astype(BF16).astype(F32)
     second = (corner - first).astype(BF16).astype(F32)
     third = corner - first - second
@@ -62,28 +81,21 @@
         near_ref[i, :, PW:] = low[i * NB : (i + 1) * NB]
 
 
-def prep(normal, jac_t):
-    rows = normal.shape[0]
+def prep_near(normal):
     return pl.pallas_call(
-        prep_kernel,
+        near_kernel,
         grid=(1,),
-        in_specs=[
-            pl.BlockSpec((rows, T), lambda i: (0, 0)),
-            pl.BlockSpec((64, PW), lambda i: (0, 0)),
-            pl.BlockSpec((64, PW), lambda i: (0, 0)),
-        ],
+        in_specs=[pl.BlockSpec((64, PW), lambda i: (0, 0))],
         out_specs=[
-            pl.BlockSpec((12, NB, PW), lambda i: (0, 0, 0)),
             pl.BlockSpec((NB, 2 * T), lambda i: (0, 0)),
             pl.BlockSpec((4, NB, 2 * PW), lambda i: (0, 0, 0)),
         ],
         out_shape=[
-            jax.ShapeDtypeStruct((12, NB, PW), BF16),
             jax.ShapeDtypeStruct((NB, 2 * T), BF16),
             jax.ShapeDtypeStruct((4, NB, 2 * PW), BF16),
         ],
         compiler_params=pltpu.CompilerParams(vmem_limit_bytes=62 << 20),
-    )(normal, normal, jac_t)
+    )(normal)
 
 
 def factor_tile(tile):
@@ -335,8 +347,9 @@
     core = lax.axis_index("core").astype(jnp.int32)[None]
     col = (lax.axis_index("y") * 8 + lax.axis_index("z")).astype(jnp.int32)[None]
     jac_t = jacobian.T
-    wide, corner, near = prep(normal, jac_t)
+    wide = prep_wide(normal, jac_t)
     wide = lax.all_gather(wide, ("y", "z"), axis=0, tiled=False)
+    corner, near = prep_near(normal)
     tiles = lax.all_to_all(jac_t.reshape(4, NB, PW), "y", 0, 0, tiled=True)
     swapped = lax.ppermute(tiles, AXES, moves(lambda r, y, z: (z, y, r)))
     near = jnp.concatenate([swapped, near], axis=2)

time: 122 us -> 122 us (level)
  blocking collectives: 26.6 us -> 17.3 us
  starting transfers between devices: 21 us -> 25.8 us
  waiting for transfers between devices: 10.4 us -> 13.8 us
  Pallas kernels: 41.4 us -> 42.7 us
    all_to_all x1 -> x0, blocking collectives: 9.42 us -> none  [per_device(): tiles = lax.all_to_all(jac_t.reshape(4, NB, PW), 'y', 0, 0, tiled=True)]
    all_to_all x0 -> x1, starting transfers between devices: none -> 5.02 us  [per_device(): tiles = lax.all_to_all(jac_t.reshape(4, NB, PW), 'y', 0, 0, tiled=True)]
    all_to_all x0 -> x1, waiting for transfers between devices: none -> 2.82 us  [per_device(): tiles = lax.all_to_all(jac_t.reshape(4, NB, PW), 'y', 0, 0, tiled=True)]
    pallas_call x1 -> x2, Pallas kernels: 2.4 us -> 3.73 us  [the longest x1 2.08 us: prep_wide(): pl.pallas_call(wide_kernel, grid=(2,), in_specs=[pl.BlockSpec((rows // 2,...]
    unnamed x23 -> x21, local copies, waits for them, and re-layouts: 4.89 us -> 4.91 us
  transfers between devices with their start and end apart: 5 -> 6, of which waited for: 4 -> 5; matrix products, arithmetic and copies ran while one was open for 3% -> 3% of each run, Pallas kernels for 23% -> 25%
where the time goes in v6:
time: 122 us
  Pallas kernels  42.7 us (35%)
  starting transfers between devices  25.8 us (21%)
  blocking collectives  17.3 us (14%)
  between operations  14.2 us (12%)
  waiting for transfers between devices  13.8 us (11%)
  local copies, waits for them, and re-layouts  7.32 us (6%)
    pallas_call x1, Pallas kernels, block(): pl.pallas_call(block_kernel, in_specs=[pl.BlockSpec(memory_space=pltpu.SM...  23.1 us
    all_to_all x1, blocking collectives, spread_over(): lax.all_to_all(jnp.broadcast_to(value[None], (count,) + value.shape), axi...  17.3 us
    all_to_all x2, starting transfers between devices, spread_over(): lax.all_to_all(jnp.broadcast_to(value[None], (count,) + value.shape), axi...  14.4 us
    pallas_call x1, Pallas kernels, last(): pl.pallas_call(last_kernel, in_specs=[there] * 3 + [whole] * 5, out_specs...  10.8 us
    ppermute x1, starting transfers between devices, per_device(): swapped = lax.ppermute(tiles, AXES, moves(lambda r, y, z: (z, y, r)))  6.36 us
    pallas_call x1, Pallas kernels, far(): pl.pallas_call(far_kernel, in_specs=[pl.BlockSpec(memory_space=pltpu.SMEM...  5.14 us
    all_to_all x1, starting transfers between devices, per_device(): tiles = lax.all_to_all(jac_t.reshape(4, NB, PW), 'y', 0, 0, tiled=True)  5.02 us
    unnamed x21, local copies, waits for them, and re-layouts  4.91 us
  transfers between devices with their start and end apart: 6, of which 5 were waited for; matrix products, arithmetic and copies ran while one was open for 3% of the time, Pallas kernels for 25%

profile of v6, /device:TPU:1, one launch (start us, length us, event | category | flops | bytes accessed | tf_op | source)
XLA Modules:
  0.0 121.8 jit_solution(14645018440624625104)
XLA Ops:
  7.2 0.0 all-gather.2.cloned.1.call-start
  7.2 2.1 %shard_map.41 = bf16[3,4,16,512]{3,2,1,0:T(8,128)(2,1)} custom-call(f32[2048,512]{1,0:T(8,128)} %normal.1, bf16[64,512]{1,0:T(8,128)(2,1)} %bitcast.jac_ref), custom_call_target="tpu_custom_call" | custom-call | tf_op jit(solution)/shard_map/pallas_call | solution.py:56
  9.3 0.0 all-gather.2.cloned.1.call-update
  9.3 5.0 %all-to-all-start = ((bf16[4,16,512]{2,1,0:T(8,128)(2,1)}), bf16[4,16,512]{2,1,0:T(8,128)(2,1)S(1)}, u32[]{:S(2)}, u32[]{:S(2)}) async-start(bf16[4,16,512]{2,1,0:T(8,128)(2,1)} %bitcast.4), calls=%async_computation | async-start | bytes 131072 | tf_op jit(solution)/shard_map/all_to_all | solution.py:353
  14.3 1.7 %shard_map.42 = (bf16[16,256]{1,0:T(8,128)(2,1)}, bf16[4,16,1024]{2,1,0:T(8,128)(2,1)}) custom-call(f32[2048,512]{1,0:T(8,128)} %normal.1), custom_call_target="tpu_custom_call" | custom-call | tf_op jit(solution)/shard_map/pallas_call | solution.py:85
  16.0 0.0 copy-start.5
  16.0 2.8 %all-to-all-done = bf16[4,16,512]{2,1,0:T(8,128)(2,1)S(1)} async-done(((bf16[4,16,512]{2,1,0:T(8,128)(2,1)}), bf16[4,16,512]{2,1,0:T(8,128)(2,1)S(1)}, u32[]{:S(2)}, u32[]{:S(2)}) %all-to-all-start) | async-done | bytes 65568 | tf_op jit(solution)/shard_map/all_to_all | solution.py:353
  18.8 0.7 pad_maximum_fusion.1
  19.5 17.3 %all_to_all.20 = bf16[8,16,768]{2,1,0:T(8,128)(2,1)S(1)} all-to-all(bf16[8,16,768]{2,1,0:T(8,128)(2,1)S(1)} %broadcast_in_dim.12), channel_id=1, replica_groups=mesh['x'=4,'core'=2,'y'=4,'z'=8] {'z'}, dimensions={0} | all-to-all | bytes 393216 | tf_op jit(solution)/shard_map/all_to_all | solution.py:339
  37.0 1.1 broadcast_in_dim.13
  38.1 4.3 %all-to-all-start.2 = ((f32[16,8,2048]{2,1,0:T(8,128)}), f32[16,8,2048]{2,1,0:T(8,128)S(1)}, u32[]{:S(2)}, u32[]{:S(2)}) async-start(f32[16,8,2048]{2,1,0:T(8,128)} %broadcast_in_dim.13), calls=%async_computation.2 | async-start | bytes 2097152 | tf_op jit(solution)/shard_map/all_to_all | solution.py:339
  42.4 6.4 %collective-permute-start.1 = (bf16[4,16,512]{2,1,0:T(8,128)(2,1)S(1)}, bf16[4,16,512]{2,1,0:T(8,128)(2,1)S(1)}, u32[]{:S(2)}, u32[]{:S(2)}) collective-permute-start(bf16[4,16,512]{2,1,0:T(8,128)(2,1)S(1)} %all-to-all-done), channel_id=1, source_target_pairs={{0,0},{1,32},{2,64},{3,96},{4,128},{5,160},{6,192},{7,224},{8,8},{... | collective-permute-start | bytes 196616 | tf_op jit(solution)/shard_map/ppermute | solution.py:354
  48.8 3.8 %collective-permute-done.1 = bf16[4,16,512]{2,1,0:T(8,128)(2,1)S(1)} collective-permute-done((bf16[4,16,512]{2,1,0:T(8,128)(2,1)S(1)}, bf16[4,16,512]{2,1,0:T(8,128)(2,1)S(1)}, u32[]{:S(2)}, u32[]{:S(2)}) %collective-permute-start.1) | collective-permute-done | bytes 65568 | tf_op jit(solution)/shard_map/ppermute | solution.py:354
  52.6 0.0 copy-done.5
  52.6 1.8 %all-to-all-done.2 = f32[16,8,2048]{2,1,0:T(8,128)S(1)} async-done(((f32[16,8,2048]{2,1,0:T(8,128)}), f32[16,8,2048]{2,1,0:T(8,128)S(1)}, u32[]{:S(2)}, u32[]{:S(2)}) %all-to-all-start.2) | async-done | bytes 1048608 | tf_op jit(solution)/shard_map/all_to_all | solution.py:339
  54.3 1.3 %broadcast_in_dim.28 = bf16[8,4,16,1536]{3,2,1,0:T(8,128)(2,1)} broadcast(bf16[4,16,1536]{2,1,0:T(8,128)(2,1)S(1)} %pad_maximum_fusion), dimensions={1,2,3} | broadcast | bytes 1769472 | tf_op jit(solution)/shard_map/broadcast_in_dim | solution.py:339
  55.7 10.1 %all-to-all-start.3 = ((bf16[8,4,16,1536]{3,2,1,0:T(8,128)(2,1)}), bf16[8,4,16,1536]{3,2,1,0:T(8,128)(2,1)S(1)}, u32[]{:S(2)}, u32[]{:S(2)}) async-start(bf16[8,4,16,1536]{3,2,1,0:T(8,128)(2,1)} %broadcast_in_dim.28), calls=%async_computation.3 | async-start | bytes 3145728 | tf_op jit(solution)/shard_map/all_to_all | solution.py:339
  65.7 0.0 collective-permute-start
  65.7 2.8 %collective-permute-done.other_ref = f32[4,4,8,2048]{3,2,1,0:T(8,128)} collective-permute-done((f32[4,4,8,2048]{3,2,1,0:T(8,128)S(1)}, f32[4,4,8,2048]{3,2,1,0:T(8,128)}, u32[]{:S(2)}, u32[]{:S(2)}) %collective-permute-start) | collective-permute-done | bytes 1048608 | tf_op jit(solution)/shard_map/ppermute | solution.py:362
  68.5 23.1 %shard_map.43 = (f32[512,512]{1,0:T(8,128)S(1)}, bf16[512,512]{1,0:T(8,128)(2,1)S(1)}) custom-call(s32[1]{0:T(128)} %bitcast.3.core_ref, f32[4,4,8,2048]{3,2,1,0:T(8,128)S(1)} %bitcast.51, f32[4,4,8,2048]{3,2,1,0:T(8,128)} %collective-permute-done.other_ref), custom_call_target="tpu_custom_call" | custom-call | tf_op jit(solution)/shard_map/pallas_call | solution.py:208
  91.6 0.0 copy-start
  91.6 1.0 copy-done
  92.6 0.0 copy-start.3
  92.6 0.8 copy-done.3
  93.4 0.0 all-to-all-done.3.near
  93.4 0.0 copy-start.1
  93.4 1.2 %copy-done.1 = f32[512,512]{1,0:T(8,128)S(1)} copy-done((f32[512,512]{1,0:T(8,128)S(1)}, f32[512,512]{1,0:T(8,128)}, u32[]{:S(2)}) %copy-start.1) | copy-done | bytes 1048600
  94.6 0.0 copy-start.4
  94.6 1.0 copy-done.4
  95.7 5.1 %shard_map.44 = (bf16[512,512]{1,0:T(8,128)(2,1)S(1)}, bf16[512,512]{1,0:T(8,128)(2,1)S(1)}, bf16[512,512]{1,0:T(8,128)(2,1)S(1)}, bf16[512,512]{1,0:T(8,128)(2,...) custom-call(s32[1]{0:T(128)} %bitcast.2.col_ref, f32[512,512]{1,0:T(8,128)S(1)} %copy-done.1, ...), custom_call_target="tpu_custom_call" | custom-call | tf_op jit(solution)/shard_map/pallas_call | solution.py:252
  100.8 0.0 copy-start.2
  100.8 0.8 copy-done.2
  101.6 2.6 %all-gather.2.cloned.1.call-done.wide = bf16[32,12,16,512]{3,2,1,0:T(8,128)(2,1)} async-done(((bf16[1,12,16,512]{3,2,1,0:T(8,128)(2,1)}), bf16[32,12,16,512]{3,2,1,0:T(8,128)(2,1)}) %all-gather.2.cloned.1.call-update) | async-done | bytes 6291472 | tf_op jit(solution)/shard_map/all_gather | solution.py:351
  104.2 10.8 %shard_map.45 = (f32[2048,512]{1,0:T(8,128)}, f32[16,2048]{1,0:T(8,128)}) custom-call(f32[2048,512]{1,0:T(8,128)} %normal.1, bf16[32,12,16,512]{3,2,1,0:T(8,128)(2,1)} %all-gather.2.cloned.1.call-done.wide, bf16[512,512]{1,0:T(8,128)(2,1)} %copy-done.2, bf16[512,512]{1,0:T(8,128)(2,1)S(1)} %get-tuple-element.19.w_hi, ...), custom_call_target="tpu_custom_call" | custom-call | tf_op jit(solution)/shard_map/pallas_call | solution.py:313
  (16 shorter events, 0.1 us)
Async XLA Ops:
  7.2 97.0 %all-gather.2.cloned.1.call-start = ((), (), s32[]{:S(2)}) async-start(), calls=%async_computation.4 | async-start | bytes 6488064 | tf_op jit(solution)/shard_map/all_gather | solution.py:351
  9.3 9.5 %all-to-all-start = ((bf16[4,16,512]{2,1,0:T(8,128)(2,1)}), bf16[4,16,512]{2,1,0:T(8,128)(2,1)S(1)}, u32[]{:S(2)}, u32[]{:S(2)}) async-start(bf16[4,16,512]{2,1,0:T(8,128)(2,1)} %bitcast.4), calls=%async_computation | async-start | bytes 131072 | tf_op jit(solution)/shard_map/all_to_all | solution.py:353
  16.0 36.6 %copy-start.5 = (bf16[4,16,1024]{2,1,0:T(8,128)(2,1)S(1)}, bf16[4,16,1024]{2,1,0:T(8,128)(2,1)}, u32[]{:S(2)}) copy-start(bf16[4,16,1024]{2,1,0:T(8,128)(2,1)} %get-tuple-element.17) | copy-start | bytes 393220
  38.1 16.3 %all-to-all-start.2 = ((f32[16,8,2048]{2,1,0:T(8,128)}), f32[16,8,2048]{2,1,0:T(8,128)S(1)}, u32[]{:S(2)}, u32[]{:S(2)}) async-start(f32[16,8,2048]{2,1,0:T(8,128)} %broadcast_in_dim.13), calls=%async_computation.2 | async-start | bytes 2097152 | tf_op jit(solution)/shard_map/all_to_all | solution.py:339
  42.4 10.2 %collective-permute-start.1 = (bf16[4,16,512]{2,1,0:T(8,128)(2,1)S(1)}, bf16[4,16,512]{2,1,0:T(8,128)(2,1)S(1)}, u32[]{:S(2)}, u32[]{:S(2)}) collective-permute-start(bf16[4,16,512]{2,1,0:T(8,128)(2,1)S(1)} %all-to-all-done), channel_id=1, source_target_pairs={{0,0},{1,32},{2,64},{3,96},{4,128},{5,160},{6,192},{7,224},{8,8},{... | collective-permute-start | bytes 196616 | tf_op jit(solution)/shard_map/ppermute | solution.py:354
  55.7 37.7 %all-to-all-start.3 = ((bf16[8,4,16,1536]{3,2,1,0:T(8,128)(2,1)}), bf16[8,4,16,1536]{3,2,1,0:T(8,128)(2,1)S(1)}, u32[]{:S(2)}, u32[]{:S(2)}) async-start(bf16[8,4,16,1536]{3,2,1,0:T(8,128)(2,1)} %broadcast_in_dim.28), calls=%async_computation.3 | async-start | bytes 3145728 | tf_op jit(solution)/shard_map/all_to_all | solution.py:339
  65.7 2.8 %collective-permute-start = (f32[4,4,8,2048]{3,2,1,0:T(8,128)S(1)}, f32[4,4,8,2048]{3,2,1,0:T(8,128)}, u32[]{:S(2)}, u32[]{:S(2)}) collective-permute-start(f32[4,4,8,2048]{3,2,1,0:T(8,128)S(1)} %bitcast.50), channel_id=1, source_target_pairs={{0,32},{1,33},{2,34},{3,35},{4,36},{5,37},{6,38},{7,39},{8,40},{9,... | collective-permute-start | bytes 3145736 | tf_op jit(solution)/shard_map/ppermute | solution.py:362
  91.6 1.0 copy-start
  92.6 0.8 copy-start.3
  93.4 1.2 %copy-start.1 = (f32[512,512]{1,0:T(8,128)S(1)}, f32[512,512]{1,0:T(8,128)}, u32[]{:S(2)}) copy-start(f32[512,512]{1,0:T(8,128)} %copy-done) | copy-start | bytes 3145732
  94.6 1.1 copy-start.4
  100.8 0.8 copy-start.2
Sparse Core Ops, SparseCore 0:
  10.6 93.5 all-gather.1

commit v7 on v5

--- a/solution.py
+++ b/solution.py
@@ -272,14 +272,14 @@
     for q in range(4):
         rows = slice(q * PW, (q + 1) * PW)
         chunks[q][0].wait()
+        if q < 3:
+            for copy in chunks[q + 1]:
+                copy.start()
         jac_rows = wide_in[8 * q : 8 * q + 8, 8:12].reshape(PW, PW)
         sums = nt(jac_rows, v_hi[...]) + nt(jac_rows, v_lo[...])
         mine = nt(own_jac[...], jac_rows)
         for copy in chunks[q][1:] + [copy_w] * (q == 0):
             copy.wait()
-        if q < 3:
-            for copy in chunks[q + 1]:
-                copy.start()
         high = wide_in[:, q].reshape(PW, PW)
         low = wide_in[:, 4 + q].reshape(PW, PW)
         drop = tn(high, w_hi[...]) + (tn(low, w_hi[...]) + tn(high, w_lo_in[...]))

time: 122 us -> 122 us (level)
  no operation moved by 1% of the time
where the time goes in v7:
time: 122 us
  Pallas kernels  41.4 us (34%)
  blocking collectives  26.6 us (22%)
  starting transfers between devices  21 us (17%)
  between operations  14.2 us (12%)
  waiting for transfers between devices  10.4 us (9%)
  local copies, waits for them, and re-layouts  7.3 us (6%)
    pallas_call x1, Pallas kernels, block(): pl.pallas_call(block_kernel, in_specs=[pl.BlockSpec(memory_space=pltpu.SM...  23.1 us
    all_to_all x1, blocking collectives, spread_over(): lax.all_to_all(jnp.broadcast_to(value[None], (count,) + value.shape), axi...  17.2 us
    all_to_all x2, starting transfers between devices, spread_over(): lax.all_to_all(jnp.broadcast_to(value[None], (count,) + value.shape), axi...  14.7 us
    pallas_call x1, Pallas kernels, last(): pl.pallas_call(last_kernel, in_specs=[there] * 3 + [whole] * 5, out_specs...  10.8 us
    all_to_all x1, blocking collectives, per_device(): tiles = lax.all_to_all(jac_t.reshape(4, NB, PW), 'y', 0, 0, tiled=True)  9.42 us
    ppermute x1, starting transfers between devices, per_device(): swapped = lax.ppermute(tiles, AXES, moves(lambda r, y, z: (z, y, r)))  6.19 us
    pallas_call x1, Pallas kernels, far(): pl.pallas_call(far_kernel, in_specs=[pl.BlockSpec(memory_space=pltpu.SMEM...  5.14 us
    unnamed x23, local copies, waits for them, and re-layouts  4.89 us
  transfers between devices with their start and end apart: 5, of which 4 were waited for; matrix products, arithmetic and copies ran while one was open for 3% of the time, Pallas kernels for 23%

profile of v7, /device:TPU:1, one launch (start us, length us, event | category | flops | bytes accessed | tf_op | source)
XLA Modules:
  0.0 121.6 jit_solution(4271827373623037638)
XLA Ops:
  7.2 0.0 all-gather.3.cloned.1.call-start
  7.2 0.0 copy-start.5
  7.2 2.4 %shard_map.41 = (bf16[12,16,512]{2,1,0:T(8,128)(2,1)}, bf16[16,256]{1,0:T(8,128)(2,1)}, bf16[4,16,1024]{2,1,0:T(8,128)(2,1)}) custom-call(f32[2048,512]{1,0:T(8,128)} %normal.1, f32[2048,512]{1,0:T(8,128)} %normal.1, bf16[64,512]{1,0:T(8,128)(2,1)} %bitcast.53), custom_call_target="tpu_custom_call" | custom-call | tf_op jit(solution)/shard_map/pallas_call | solution.py:67
  9.6 0.0 copy-start.6
  9.6 0.0 all-gather.3.cloned.1.call-update
  9.6 0.0 copy-done.5
  9.7 9.4 %all_to_all.20 = bf16[4,16,512]{2,1,0:T(8,128)(2,1)S(1)} all-to-all(bf16[4,16,512]{2,1,0:T(8,128)(2,1)S(1)} %bitcast.54), channel_id=1, replica_groups=mesh['x'=4,'core'=2,'y'=4,'z'=8] {'y'}, dimensions={0} | all-to-all | bytes 131072 | tf_op jit(solution)/shard_map/all_to_all | solution.py:340
  19.1 0.7 pad_maximum_fusion.1
  19.8 17.2 %all_to_all.21 = bf16[8,16,768]{2,1,0:T(8,128)(2,1)S(1)} all-to-all(bf16[8,16,768]{2,1,0:T(8,128)(2,1)S(1)} %broadcast_in_dim.12), channel_id=1, replica_groups=mesh['x'=4,'core'=2,'y'=4,'z'=8] {'z'}, dimensions={0} | all-to-all | bytes 393216 | tf_op jit(solution)/shard_map/all_to_all | solution.py:327
  37.1 1.1 broadcast_in_dim.13
  38.2 4.8 %all-to-all-start.2 = ((f32[16,8,2048]{2,1,0:T(8,128)}), f32[16,8,2048]{2,1,0:T(8,128)S(1)}, u32[]{:S(2)}, u32[]{:S(2)}) async-start(f32[16,8,2048]{2,1,0:T(8,128)} %broadcast_in_dim.13), calls=%async_computation.2 | async-start | bytes 2097152 | tf_op jit(solution)/shard_map/all_to_all | solution.py:327
  42.9 6.2 %collective-permute-start.1 = (bf16[4,16,512]{2,1,0:T(8,128)(2,1)S(1)}, bf16[4,16,512]{2,1,0:T(8,128)(2,1)S(1)}, u32[]{:S(2)}, u32[]{:S(2)}) collective-permute-start(bf16[4,16,512]{2,1,0:T(8,128)(2,1)S(1)} %all_to_all.20), channel_id=1, source_target_pairs={{0,0},{1,32},{2,64},{3,96},{4,128},{5,160},{6,192},{7,224},{8,8},{... | collective-permute-start | bytes 196616 | tf_op jit(solution)/shard_map/ppermute | solution.py:341
  49.1 3.6 %collective-permute-done.1 = bf16[4,16,512]{2,1,0:T(8,128)(2,1)S(1)} collective-permute-done((bf16[4,16,512]{2,1,0:T(8,128)(2,1)S(1)}, bf16[4,16,512]{2,1,0:T(8,128)(2,1)S(1)}, u32[]{:S(2)}, u32[]{:S(2)}) %collective-permute-start.1) | collective-permute-done | bytes 65568 | tf_op jit(solution)/shard_map/ppermute | solution.py:341
  52.7 0.0 copy-done.6
  52.7 2.2 %all-to-all-done.2 = f32[16,8,2048]{2,1,0:T(8,128)S(1)} async-done(((f32[16,8,2048]{2,1,0:T(8,128)}), f32[16,8,2048]{2,1,0:T(8,128)S(1)}, u32[]{:S(2)}, u32[]{:S(2)}) %all-to-all-start.2) | async-done | bytes 1048608 | tf_op jit(solution)/shard_map/all_to_all | solution.py:327
  54.9 1.3 %broadcast_in_dim.28 = bf16[8,4,16,1536]{3,2,1,0:T(8,128)(2,1)} broadcast(bf16[4,16,1536]{2,1,0:T(8,128)(2,1)S(1)} %pad_maximum_fusion), dimensions={1,2,3} | broadcast | bytes 1769472 | tf_op jit(solution)/shard_map/broadcast_in_dim | solution.py:327
  56.2 9.9 %all-to-all-start.3 = ((bf16[8,4,16,1536]{3,2,1,0:T(8,128)(2,1)}), bf16[8,4,16,1536]{3,2,1,0:T(8,128)(2,1)S(1)}, u32[]{:S(2)}, u32[]{:S(2)}) async-start(bf16[8,4,16,1536]{3,2,1,0:T(8,128)(2,1)} %broadcast_in_dim.28), calls=%async_computation.3 | async-start | bytes 3145728 | tf_op jit(solution)/shard_map/all_to_all | solution.py:327
  66.2 0.0 collective-permute-start
  66.2 2.8 %collective-permute-done.other_ref = f32[4,4,8,2048]{3,2,1,0:T(8,128)} collective-permute-done((f32[4,4,8,2048]{3,2,1,0:T(8,128)S(1)}, f32[4,4,8,2048]{3,2,1,0:T(8,128)}, u32[]{:S(2)}, u32[]{:S(2)}) %collective-permute-start) | collective-permute-done | bytes 1048608 | tf_op jit(solution)/shard_map/ppermute | solution.py:349
  69.0 23.1 %shard_map.42 = (f32[512,512]{1,0:T(8,128)S(1)}, bf16[512,512]{1,0:T(8,128)(2,1)S(1)}) custom-call(s32[1]{0:T(128)} %bitcast.3.core_ref, f32[4,4,8,2048]{3,2,1,0:T(8,128)S(1)} %bitcast.51, f32[4,4,8,2048]{3,2,1,0:T(8,128)} %collective-permute-done.other_ref), custom_call_target="tpu_custom_call" | custom-call | tf_op jit(solution)/shard_map/pallas_call | solution.py:196
  92.0 0.0 copy-start
  92.1 1.0 copy-done
  93.0 0.0 copy-start.3
  93.0 0.8 copy-done.3
  93.8 0.0 all-to-all-done.3.near
  93.8 0.0 copy-start.1
  93.8 1.2 %copy-done.1 = f32[512,512]{1,0:T(8,128)S(1)} copy-done((f32[512,512]{1,0:T(8,128)S(1)}, f32[512,512]{1,0:T(8,128)}, u32[]{:S(2)}) %copy-start.1) | copy-done | bytes 1048600
  95.1 0.0 copy-start.4
  95.1 1.0 copy-done.4
  96.1 5.1 %shard_map.43 = (bf16[512,512]{1,0:T(8,128)(2,1)S(1)}, bf16[512,512]{1,0:T(8,128)(2,1)S(1)}, bf16[512,512]{1,0:T(8,128)(2,1)S(1)}, bf16[512,512]{1,0:T(8,128)(2,...) custom-call(s32[1]{0:T(128)} %bitcast.2.col_ref, f32[512,512]{1,0:T(8,128)S(1)} %copy-done.1, ...), custom_call_target="tpu_custom_call" | custom-call | tf_op jit(solution)/shard_map/pallas_call | solution.py:240
  101.3 0.0 copy-start.2
  101.3 0.8 copy-done.2
  102.1 1.9 %all-gather.3.cloned.1.call-done = bf16[384,16,512]{2,1,0:T(8,128)(2,1)} async-done(((bf16[12,16,512]{2,1,0:T(8,128)(2,1)}), bf16[384,16,512]{2,1,0:T(8,128)(2,1)}) %all-gather.3.cloned.1.call-update) | async-done | bytes 6291472 | tf_op jit(solution)/shard_map/all_gather | solution.py:339
  103.9 10.8 %shard_map.44 = (f32[2048,512]{1,0:T(8,128)}, f32[16,2048]{1,0:T(8,128)}) custom-call(f32[2048,512]{1,0:T(8,128)} %normal.1, bf16[32,12,16,512]{3,2,1,0:T(8,128)(2,1)} %bitcast.52, bf16[512,512]{1,0:T(8,128)(2,1)} %copy-done.2, bf16[512,512]{1,0:T(8,128)(2,1)S(1)} %get-tuple-element.21.w_hi, bf16[512,512]{1,0:T(8,128)(2,1)S(1)} %get-tuple-element.22.v_hi, ...), custom_call_target="tpu_custom_call" | custom-call | tf_op jit(solution)/shard_map/pallas_call | solution.py:301
  (16 shorter events, 0.1 us)
Async XLA Ops:
  7.2 96.8 %all-gather.3.cloned.1.call-start = ((), (), s32[]{:S(2)}) async-start(), calls=%async_computation.4 | async-start | bytes 6488064 | tf_op jit(solution)/shard_map/all_gather | solution.py:339
  7.2 2.4 %copy-start.5 = (bf16[512,64]{0,1:T(8,128)(2,1)S(1)}, bf16[512,64]{0,1:T(8,128)(2,1)}, u32[]{:S(2)}) copy-start(bf16[512,64]{0,1:T(8,128)(2,1)} %param.3) | copy-start | bytes 196612
  9.6 43.1 %copy-start.6 = (bf16[4,16,1024]{2,1,0:T(8,128)(2,1)S(1)}, bf16[4,16,1024]{2,1,0:T(8,128)(2,1)}, u32[]{:S(2)}) copy-start(bf16[4,16,1024]{2,1,0:T(8,128)(2,1)} %get-tuple-element.19) | copy-start | bytes 393220
  38.2 16.7 %all-to-all-start.2 = ((f32[16,8,2048]{2,1,0:T(8,128)}), f32[16,8,2048]{2,1,0:T(8,128)S(1)}, u32[]{:S(2)}, u32[]{:S(2)}) async-start(f32[16,8,2048]{2,1,0:T(8,128)} %broadcast_in_dim.13), calls=%async_computation.2 | async-start | bytes 2097152 | tf_op jit(solution)/shard_map/all_to_all | solution.py:327
  42.9 9.8 %collective-permute-start.1 = (bf16[4,16,512]{2,1,0:T(8,128)(2,1)S(1)}, bf16[4,16,512]{2,1,0:T(8,128)(2,1)S(1)}, u32[]{:S(2)}, u32[]{:S(2)}) collective-permute-start(bf16[4,16,512]{2,1,0:T(8,128)(2,1)S(1)} %all_to_all.20), channel_id=1, source_target_pairs={{0,0},{1,32},{2,64},{3,96},{4,128},{5,160},{6,192},{7,224},{8,8},{... | collective-permute-start | bytes 196616 | tf_op jit(solution)/shard_map/ppermute | solution.py:341
  56.2 37.6 %all-to-all-start.3 = ((bf16[8,4,16,1536]{3,2,1,0:T(8,128)(2,1)}), bf16[8,4,16,1536]{3,2,1,0:T(8,128)(2,1)S(1)}, u32[]{:S(2)}, u32[]{:S(2)}) async-start(bf16[8,4,16,1536]{3,2,1,0:T(8,128)(2,1)} %broadcast_in_dim.28), calls=%async_computation.3 | async-start | bytes 3145728 | tf_op jit(solution)/shard_map/all_to_all | solution.py:327
  66.2 2.8 %collective-permute-start = (f32[4,4,8,2048]{3,2,1,0:T(8,128)S(1)}, f32[4,4,8,2048]{3,2,1,0:T(8,128)}, u32[]{:S(2)}, u32[]{:S(2)}) collective-permute-start(f32[4,4,8,2048]{3,2,1,0:T(8,128)S(1)} %bitcast.50), channel_id=1, source_target_pairs={{0,32},{1,33},{2,34},{3,35},{4,36},{5,37},{6,38},{7,39},{8,40},{9,... | collective-permute-start | bytes 3145736 | tf_op jit(solution)/shard_map/ppermute | solution.py:349
  92.0 1.0 copy-start
  93.0 0.8 copy-start.3
  93.8 1.2 %copy-start.1 = (f32[512,512]{1,0:T(8,128)S(1)}, f32[512,512]{1,0:T(8,128)}, u32[]{:S(2)}) copy-start(f32[512,512]{1,0:T(8,128)} %copy-done) | copy-start | bytes 3145732
  95.1 1.1 copy-start.4
  101.3 0.8 copy-start.2
Sparse Core Ops, SparseCore 0:
  10.6 93.3 all-gather.2
